TPU v7x, 256 devices: a whole 4x4x8 slice. The times are simulated.
256 devices in a mesh: rep: 4 (over z_lo, core), fsdp: 64 (over y, z_hi, x).
Axes of the slice: x: 4, y: 4, z: 8 (z_hi: 4, z_lo: 2; z = z_hi * 2 + z_lo), core: 2. Of those that a mesh axis runs over, the one named last changes fastest.
Arguments:
- tokens: bfloat16 [32768, 4096], P(('rep', 'fsdp')), may hold values from -24 to 24
- left_factor: bfloat16 [4096, 256], P('fsdp'), may hold values from -0.09375 to 0.09375
- right_factor: bfloat16 [256, 14336], P(None, 'fsdp'), may hold values from -0.375 to 0.375
- tile_values: bfloat16 [128, 128, 128], P('fsdp'), may hold values from -0.5 to 0.5
- tile_rows: int32 [128], P('fsdp'), may hold values from 0 to 31
- tile_cols: int32 [128], P('fsdp'), may hold values from 0 to 111
- grad_out: bfloat16 [32768, 14336], P(('rep', 'fsdp')), may hold values from -6 to 6
Outputs:
- out_rows: bfloat16 [32768, 14336], P(('rep', 'fsdp'))
- input_grad: bfloat16 [32768, 4096], P(('rep', 'fsdp'))
- left_grad: float32 [4096, 256], P('fsdp')
- right_grad: float32 [256, 14336], P(None, 'fsdp')
- tile_grad: float32 [128, 128, 128], P('fsdp')
All inputs are finite; a program needn't handle non-finite values.
Results may differ from a plain program's by a relative error of at most 0.0038.
Values may be sent and summed in bfloat16 or wider, within the bound.
A program may use at most 192 MiB of HBM per device.

v0:
```python
import math

import jax
import jax.numpy as jnp
from jax import lax
from jax.sharding import PartitionSpec as P

D = 4096
FF = 14336
TB = 128


def contract_rows(left, right):
    return lax.dot_general(
        left, right, (((0,), (0,)), ((), ())), preferred_element_type=jnp.float32
    )


def contract_cols(left, right):
    return lax.dot_general(
        left, right, (((1,), (1,)), ((), ())), preferred_element_type=jnp.float32
    )


def local(tokens, left_factor, right_factor, tile_values, tile_rows, tile_cols, grad_out):
    fsdp_count = lax.axis_size("fsdp")
    rep_count = lax.axis_size("rep")
    rows_here = tokens.shape[0]
    grad_scale = 1.0 / math.sqrt(rows_here * fsdp_count * rep_count)
    row_blocks = D // TB
    col_blocks = FF // TB
    left_all, tiles_all, rows_all, cols_all = (
        lax.all_gather(left_factor, "fsdp", axis=0, tiled=True),
        lax.all_gather(tile_values, "fsdp", axis=0, tiled=True),
        lax.all_gather(tile_rows, "fsdp", axis=0, tiled=True),
        lax.all_gather(tile_cols, "fsdp", axis=0, tiled=True),
    )
    right_all = lax.all_gather(right_factor, "fsdp", axis=1, tiled=True)
    latent = jnp.dot(tokens, left_all, preferred_element_type=jnp.float32).astype(jnp.bfloat16)
    token_tiles = jnp.take(tokens.reshape(rows_here, row_blocks, TB), rows_all, axis=1)
    tile_prod = jnp.einsum(
        "tkc,kcd->tkd", token_tiles, tiles_all, preferred_element_type=jnp.float32
    )
    sparse_out = (
        jnp.zeros((rows_here, col_blocks, TB), jnp.float32)
        .at[:, cols_all]
        .add(tile_prod)
        .reshape(rows_here, FF)
    )
    out_rows = (jnp.dot(latent, right_all, preferred_element_type=jnp.float32) + sparse_out).astype(
        jnp.bfloat16
    )
    latent_grad = contract_cols(grad_out, right_all).astype(jnp.bfloat16)
    grad_tiles = jnp.take(grad_out.reshape(rows_here, col_blocks, TB), cols_all, axis=1)
    tile_back = jnp.einsum(
        "tkd,kcd->tkc", grad_tiles, tiles_all, preferred_element_type=jnp.float32
    )
    sparse_back = (
        jnp.zeros((rows_here, row_blocks, TB), jnp.float32)
        .at[:, rows_all]
        .add(tile_back)
        .reshape(rows_here, D)
    )
    input_grad = (contract_cols(latent_grad, left_all) + sparse_back).astype(jnp.bfloat16)
    left_part = contract_rows(tokens, latent_grad) * grad_scale
    tile_part = (
        jnp.einsum("tkc,tkd->kcd", token_tiles, grad_tiles, preferred_element_type=jnp.float32)
        * grad_scale
    )
    grad_cols = lax.all_to_all(grad_out, "fsdp", split_axis=1, concat_axis=0, tiled=True)
    right_part = (
        contract_rows(lax.all_gather(latent, "fsdp", axis=0, tiled=True), grad_cols) * grad_scale
    )
    tile_flat = tile_part.reshape(-1, TB)
    left_shard, tile_shard = (
        lax.psum_scatter(left_part, "fsdp", scatter_dimension=0, tiled=True),
        lax.psum_scatter(tile_flat, "fsdp", scatter_dimension=0, tiled=True),
    )
    left_grad, right_grad, tile_grad = lax.psum((left_shard, right_part, tile_shard), "rep")
    return (out_rows, input_grad, left_grad, right_grad, tile_grad.reshape(-1, TB, TB))


def solution(mesh):
    placed = (
        P(("rep", "fsdp"), None),
        P("fsdp", None),
        P(None, "fsdp"),
        P("fsdp", None, None),
        P("fsdp"),
        P("fsdp"),
        P(("rep", "fsdp"), None),
    )
    return jax.shard_map(
        local,
        mesh=mesh,
        in_specs=placed,
        out_specs=(
            P(("rep", "fsdp"), None),
            P(("rep", "fsdp"), None),
            P("fsdp", None),
            P(None, "fsdp"),
            P("fsdp", None, None),
        ),
        check_vma=False,
    )
```

profile of v0, /device:TPU:1, one launch (start us, length us, event | category | flops | bytes accessed | tf_op | source)
XLA Modules:
  0.0 1287.6 jit_solution(9276882917544199490)
XLA Ops:
  7.2 0.7 all-gather.5.cloned.1.call-update
  7.9 0.7 all-gather.7.cloned.1.call-update
  9.4 82.7 %all-gather.5.cloned.1.call-done = bf16[4096,256]{1,0:T(8,128)(2,1)} async-done(((bf16[64,256]{1,0:T(8,128)(2,1)}), bf16[4096,256]{1,0:T(8,128)(2,1)}) %all-gather.5.cloned.1.call-update) | async-done | bytes 2097168 | tf_op jit(solution)/shard_map/all_gather | solution.py:33
  92.2 3.0 convolution_convert_fusion
  95.2 105.7 %all-gather.7.cloned.1.call-done = bf16[256,14336]{0,1:T(8,128)(2,1)} async-done(((bf16[256,224]{0,1:T(8,128)(2,1)}), bf16[256,14336]{0,1:T(8,128)(2,1)}) %all-gather.7.cloned.1.call-update) | async-done | bytes 7340048 | tf_op jit(solution)/shard_map/all_gather | solution.py:38
  201.0 5.3 convolution_convert_fusion.1
  206.3 2.7 fusion.1
  209.0 5.6 copy.45
  214.7 6.1 copy.37
  221.5 6.0 copy.38
  229.9 22.3 %all-reduce.2 = (s32[128]{0:T(128)S(1)}, s32[128]{0:T(128)S(1)}) all-reduce(s32[128]{0:T(128)S(1)} %dynamic-update-slice, s32[128]{0:T(128)S(1)} %dynamic-update-slice.1), channel_id=1, replica_groups=mesh['rep'=4,'fsdp'=64] {'fsdp'}, use_global_device_ids=true, to_apply=%add | all-reduce | flops 256 | bytes 2048
  252.3 5.3 gather_fusion.1
  257.5 3.1 gather_fusion
  260.6 8.7 broadcast_multiply_fusion
  269.3 6.5 all-to-all-start
  276.0 46.4 %all-gather.9.cloned.1.call-done = bf16[128,128,128]{2,1,0:T(8,128)(2,1)} async-done(((bf16[2,128,128]{2,1,0:T(8,128)(2,1)}), bf16[128,128,128]{2,1,0:T(8,128)(2,1)}) %all-gather.9.cloned.1.call-update) | async-done | bytes 4194320 | tf_op jit(solution)/shard_map/all_gather | solution.py:34
  322.4 9.8 fusion.5
  332.4 17.1 %scatter_fusion.1 = f32[128,32,128]{2,0,1:T(8,128)S(1)} fusion(f32[128,32,128]{2,0,1:T(8,128)S(1)} %broadcast_in_dim.35, s32[128]{0:T(128)S(1)} %get-tuple-element.30, f32[128,128,128]{2,1,0:T(8,128)} %fusion.5), kind=kCustom, calls=%fused_computation.3 | custom fusion | flops 2097152 | bytes 25166336 | tf_op jit(solution)/shard_map/scatter-add | solution.py:61
  349.5 8.0 fusion.8
  357.5 3.9 broadcast_in_dim.30
  361.5 26.3 %scatter_fusion = f32[128,112,128]{2,0,1:T(8,128)} fusion(f32[128,112,128]{2,0,1:T(8,128)} %broadcast_in_dim.30, s32[128]{0:T(128)S(1)} %get-tuple-element.31, f32[128,128,128]{2,1,0:T(8,128)} %fusion.8), kind=kCustom, calls=%fused_computation.2 | custom fusion | flops 2097152 | bytes 25166336 | tf_op jit(solution)/shard_map/scatter-add | solution.py:47
  387.8 55.2 %all-gather.11.cloned.1.call-done = bf16[8192,256]{1,0:T(8,128)(2,1)} async-done(((bf16[128,256]{1,0:T(8,128)(2,1)}), bf16[8192,256]{1,0:T(8,128)(2,1)}) %all-gather.11.cloned.1.call-update) | async-done | bytes 4194320 | tf_op jit(solution)/shard_map/all_gather | solution.py:72
  443.0 5.2 fusion.17
  448.3 1.8 fusion.2
  450.1 336.4 %reduce-scatter.7.cloned.1.call-done = f32[64,256]{1,0:T(8,128)} async-done(((f32[4096,256]{1,0:T(8,128)}), f32[64,256]{1,0:T(8,128)}) %reduce-scatter.7.cloned.1.call-update) | async-done | bytes 65552
  786.5 1.6 copy.46
  788.1 398.4 %reduce-scatter.5.cloned.1.call-done = f32[256,128]{1,0:T(8,128)} async-done(((f32[16384,128]{1,0:T(8,128)}), f32[256,128]{1,0:T(8,128)}) %reduce-scatter.5.cloned.1.call-update) | async-done | bytes 131088 | tf_op jit(solution)/shard_map/reduce_scatter | solution.py:77
  1186.6 9.5 fusion
  1196.1 79.8 %all-reduce.6.cloned.1.call-done = (f32[64,256]{0,1:T(8,128)}, f32[256,224]{0,1:T(8,128)}, f32[2,128,128]{2,1,0:T(8,128)}) async-done(((f32[64,256]{0,1:T(8,128)}, f32[256,224]{0,1:T(8,128)}, f32[2,128,128]{2,1,0:T(8,128)}), (f32[64,256]{0,1:T(8,128)}, f32[256,224]{0,1:T(8,128)}, f32[2,128,128]{2,1,0:T(8,128)})) %all-reduce.6.cloned.1.call-update) | async-done | bytes 426000 | tf_op jit(solution)/shard_map/psum | solution.py:79
  1276.0 1.6 copy.43
  1277.6 1.6 copy.65
  1279.2 1.6 copy.66
  (37 shorter events, 3.9 us)
Async XLA Ops:
  7.2 85.0 %all-gather.5.cloned.1.call-start = ((), (), s32[]{:S(2)}) async-start(), calls=%async_computation.3 | async-start | bytes 2129920 | tf_op jit(solution)/shard_map/all_gather | solution.py:33
  7.9 193.1 %all-gather.7.cloned.1.call-start = ((), (), s32[]{:S(2)}) async-start(), calls=%async_computation.4 | async-start | bytes 7454720 | tf_op jit(solution)/shard_map/all_gather | solution.py:38
  8.6 313.8 %all-gather.9.cloned.1.call-start = ((), (), s32[]{:S(2)}) async-start(), calls=%async_computation.5 | async-start | bytes 4259840 | tf_op jit(solution)/shard_map/all_gather | solution.py:34
  9.4 433.6 %all-gather.11.cloned.1.call-start = ((), (), s32[]{:S(2)}) async-start(), calls=%async_computation.6 | async-start | bytes 4259840 | tf_op jit(solution)/shard_map/all_gather | solution.py:72
  95.2 111.1 %copy-start = (bf16[128,4096]{1,0:T(8,128)(2,1)S(1)}, bf16[128,4096]{1,0:T(8,128)(2,1)}, u32[]{:S(2)}) copy-start(bf16[128,4096]{1,0:T(8,128)(2,1)} %param.7) | copy-start | bytes 3145732
  95.2 691.3 %reduce-scatter.7.cloned.1.call-start = ((), (), s32[]{:S(2)}) async-start(), calls=%async_computation.8 | async-start | bytes 4259840
  214.6 971.9 %reduce-scatter.5.cloned.1.call-start = ((), (), s32[]{:S(2)}) async-start(), calls=%async_computation.7 | async-start | bytes 8519680 | tf_op jit(solution)/shard_map/reduce_scatter | solution.py:77
  221.4 6.7 copy-start.5
  221.4 8.0 copy-start.3
  221.4 8.2 copy-start.4
  269.3 118.4 %all-to-all-start = ((bf16[128,64,224]{0,2,1:T(8,128)(2,1)}), bf16[128,64,224]{0,2,1:T(8,128)(2,1)}, u32[]{:S(2)}, u32[]{:S(2)}) async-start(bf16[128,64,224]{0,2,1:T(8,128)(2,1)} %bitcast.58), calls=%async_computation | async-start | bytes 7340032 | tf_op jit(solution)/shard_map/all_to_all | solution.py:70
  275.8 1000.1 %all-reduce.6.cloned.1.call-start = ((), (), s32[]{:S(2)}) async-start(), calls=%async_computation.9 | async-start | bytes 983040 | tf_op jit(solution)/shard_map/psum | solution.py:79
  443.0 5.2 copy-start.1
  448.3 738.3 %copy-start.2 = (bf16[128,256]{1,0:T(8,128)(2,1)S(1)}, bf16[128,256]{1,0:T(8,128)(2,1)}, u32[]{:S(2)}) copy-start(bf16[128,256]{1,0:T(8,128)(2,1)} %convolution_convert_fusion) | copy-start | bytes 196612
Sparse Core Ops, SparseCore 0:
  11.3 80.8 all-gather.4
  95.5 105.4 all-gather.6
  204.3 118.0 all-gather.8
  326.1 116.8 all-gather.10
  445.4 341.1 reduce-scatter.6
  789.1 397.4 reduce-scatter.4
  1190.2 85.6 all-reduce.5
where the time goes:
time: 1290 us
  waiting for transfers between devices  1110 us (86%)
  matrix products  54.1 us (4%)
  other arithmetic  43.4 us (3%)
  local copies, waits for them, and re-layouts  39 us (3%)
  blocking collectives  22.3 us (2%)
  between operations  14.9 us (1%)
    reduce_scatter x1, waiting for transfers between devices, local(): lax.psum_scatter(tile_flat, 'fsdp', scatter_dimension=0, tiled=True)  398 us
    unnamed x8, waiting for transfers between devices  339 us
    all_gather x1, waiting for transfers between devices, local(): right_all = lax.all_gather(right_factor, 'fsdp', axis=1, tiled=True)  106 us
    all_gather x1, waiting for transfers between devices, local(): lax.all_gather(left_factor, 'fsdp', axis=0, tiled=True)  82.7 us
    psum x1, waiting for transfers between devices, local(): lax.psum((left_shard, right_part, tile_shard), 'rep')  79.8 us
    all_gather x1, waiting for transfers between devices, local(): lax.all_gather(latent, 'fsdp', axis=0, tiled=True)  55.2 us
    all_gather x1, waiting for transfers between devices, local(): lax.all_gather(tile_values, 'fsdp', axis=0, tiled=True)  46.4 us
    scatter-add x1, other arithmetic, local(): sparse_out = jnp.zeros((rows_here, col_blocks, TB), jnp.float32).at[:, co...  26.3 us
  transfers between devices with their start and end apart: 8, of which 7 were waited for; matrix products, arithmetic and copies ran while one was open for 10% of the time, Pallas kernels for 0%

commit v1 on v0

v1 whole, which is shorter than its diff:
```python
import math

import jax
import jax.numpy as jnp
from jax import lax
from jax.experimental import pallas as pl
from jax.experimental.pallas import tpu as pltpu
from jax.sharding import PartitionSpec as P

D = 4096
FF = 14336
TB = 128
R = 256
SIDE = 4
LEFT = 64
RIGHT = 224
GROWS = LEFT + RIGHT + TB + 16
QROWS = LEFT + RIGHT + TB
MESH = pl.DeviceIdType.MESH
BF = jnp.bfloat16
F32 = jnp.float32
Y, H, X = 0, 1, 2
ANY = pl.BlockSpec(memory_space=pl.ANY)
VMEM = pl.BlockSpec(memory_space=pltpu.VMEM)


class Place:
    def __init__(self):
        rep, f = lax.axis_index("rep"), lax.axis_index("fsdp")
        self.l, self.c = rep // 2, rep % 2
        self.at = [f // 16, (f // 4) % 4, f % 4]
        self.s = 2 * self.l - 1
        self.sib = self.dev(core=1 - self.c)
        self.pair = self.dev(low=1 - self.l)
        self.out = self.dev(low=1 - self.l, step=(H, self.s))
        self.plus = {a: self.dev(step=(a, 1)) for a in (Y, X)}
        self.minus = {a: self.dev(step=(a, 3)) for a in (Y, X)}

    def dev(self, core=None, low=None, step=None):
        core = self.c if core is None else core
        low = self.l if low is None else low
        at = list(self.at)
        if step:
            at[step[0]] = (at[step[0]] + step[1] + 4) % 4
        return {"rep": low * 2 + core, "fsdp": (at[0] * 4 + at[1]) * 4 + at[2]}

    def greet(self):
        barrier = pltpu.get_barrier_semaphore()
        near = [self.sib, self.pair, self.out] + [d[a] for d in (self.plus, self.minus) for a in (Y, X)]
        for device in near:
            pl.semaphore_signal(barrier, inc=1, device_id=device, device_id_type=MESH)
        pl.semaphore_wait(barrier, len(near))


class Wire:
    def __init__(self, send_sems, recv_sems):
        self.send_sems, self.recv_sems = send_sems, recv_sems
        self.started = []

    def __call__(self, src, dst, device):
        k = len(self.started)
        copy = pltpu.make_async_remote_copy(
            src_ref=src,
            dst_ref=dst,
            send_sem=self.send_sems.at[k],
            recv_sem=self.recv_sems.at[k],
            device_id=device,
            device_id_type=MESH,
        )
        copy.start()
        self.started.append(copy)
        return copy

    def finish(self):
        for copy in self.started:
            copy.wait_send()


def interleave(parts):
    parts = list(parts)
    while parts:
        for part in list(parts):
            try:
                next(part)
            except StopIteration:
                parts.remove(part)


def view(ref, fixed, axis, j, row0, rows, half=None, chunk=None, chunks=1):
    sel = list(fixed)
    sel[axis] = j
    r0, n = row0, rows
    free = [a for a in range(3) if a != axis and fixed[a] is None]
    if half is not None:
        if free:
            width = 2 // chunks
            start = half * 2 + (0 if chunk is None else chunk * width)
            sel[free[0]] = pl.ds(start, width if chunk is not None else 2)
        elif rows % 32 == 0:
            n = rows // 2
            r0 = row0 + half * n
        else:
            cut = (rows // 32 + 1) * 16
            r0, n = (row0, cut) if half == 0 else (row0 + cut, rows - cut)
    sel = [slice(None) if v is None else v for v in sel]
    return ref.at[sel[0], sel[1], sel[2], pl.ds(r0, n), :]


GATHER = (((X, Y, H), 0, 144), ((Y, H, X), 144, 160), ((H, X, Y), 304, 128))


def gather_kernel(pay, tok, grad, full, tok_s, grad_s, send_sems, recv_sems, local_sem, side_sems, wide_sems):
    me = Place()
    mine = full.at[me.c]
    own = pltpu.make_async_copy(pay.at[me.c], mine.at[me.at[0], me.at[1], me.at[2]], local_sem)
    own.start()
    me.greet()
    wire = Wire(send_sems, recv_sems)

    def to_sibling(src, dst, pair):
        return pltpu.make_async_remote_copy(
            src_ref=src,
            dst_ref=dst,
            send_sem=pair.at[0],
            recv_sem=pair.at[1],
            device_id=me.sib,
            device_id_type=MESH,
        )

    def part(order, row0, rows):
        for stage, axis in enumerate(order):
            fixed = [None if a in order[:stage] else me.at[a] for a in range(3)]
            last = stage == 2

            def blk(j, half=None, chunk=None, chunks=1):
                return view(mine, fixed, axis, j, row0, rows, half, chunk, chunks)

            def src(j, half, chunk=None, chunks=1):
                if stage:
                    return blk(j, half, chunk, chunks)
                return view(pay.at[pl.ds(me.c, 1)].reshape(1, 1, 1, GROWS, TB), [0, 0, 0], axis, 0, row0, rows, half)

            def got(ref):
                if last:
                    to_sibling(ref, ref, side_sems).start()

            def send(j, half, device, chunk=None, chunks=1, first=False):
                ref = blk(j, half, chunk, chunks)
                return wire(ref, ref, device)

            i = me.at[axis]
            if last:
                got(blk(i))
            if axis == H:
                l, s = me.l, me.s
                up, down, across = (i + s + 4) % 4, (i - s + 4) % 4, (i + 2) % 4
                chunks = 2 if last else 1
                ids = range(chunks) if last else (None,)
                a = [send(i, 1 - l, me.out, q, chunks) for q in ids]
                b = [send(i, l, me.out, q, chunks) for q in ids]
                yield
                f = []
                for k, q in enumerate(ids):
                    a[k].wait_recv()
                    f.append(send(up, l, me.pair, q, chunks))
                    got(blk(up, l, q, chunks))
                yield
                e = []
                for k, q in enumerate(ids):
                    b[k].wait_recv()
                    e.append(send(up, 1 - l, me.pair, q, chunks))
                    got(blk(up, 1 - l, q, chunks))
                yield
                g = []
                for k, q in enumerate(ids):
                    f[k].wait_recv()
                    g.append(send(down, 1 - l, me.out, q, chunks))
                    got(blk(down, 1 - l, q, chunks))
                yield
                for k, q in enumerate(ids):
                    e[k].wait_recv()
                    got(blk(down, l, q, chunks))
                w = []
                for k, q in enumerate(ids):
                    g[k].wait_recv()
                    w.append(send(across, l, me.pair, q, chunks))
                    got(blk(across, l, q, chunks))
                yield
                for k, q in enumerate(ids):
                    w[k].wait_recv()
                    got(blk(across, 1 - l, q, chunks))
            else:
                plus, minus = me.plus[axis], me.minus[axis]
                after, before, across = (i + 1) % 4, (i + 3) % 4, (i + 2) % 4
                a0, b1 = send(i, 0, plus), send(i, 1, minus)
                a1, b0 = send(i, 1, plus), send(i, 0, minus)
                yield
                a0.wait_recv()
                c0 = send(before, 0, plus)
                got(blk(before, 0))
                b1.wait_recv()
                c1 = send(after, 1, minus)
                got(blk(after, 1))
                yield
                a1.wait_recv()
                got(blk(before, 1))
                b0.wait_recv()
                got(blk(after, 0))
                yield
                c0.wait_recv()
                got(blk(across, 0))
                c1.wait_recv()
                got(blk(across, 1))

    own.wait()
    runs = [part(*p) for p in GATHER]
    for run in runs:
        next(run)
    swaps = [to_sibling(tok, tok_s, wide_sems.at[0]), to_sibling(grad, grad_s, wide_sems.at[1])]
    for swap in swaps:
        swap.start()
    interleave(runs)
    wire.finish()
    for swap in swaps:
        swap.wait()
    whole = to_sibling(mine, full.at[1 - me.c], side_sems)
    whole.wait()


def gather(pay, tok, grad):
    return pl.pallas_call(
        gather_kernel,
        out_shape=(
            jax.ShapeDtypeStruct((2, SIDE, SIDE, SIDE, GROWS, TB), BF),
            jax.ShapeDtypeStruct(tok.shape, BF),
            jax.ShapeDtypeStruct(grad.shape, BF),
        ),
        in_specs=[ANY] * 3,
        out_specs=(ANY,) * 3,
        scratch_shapes=[
            pltpu.SemaphoreType.DMA((80,)),
            pltpu.SemaphoreType.DMA((80,)),
            pltpu.SemaphoreType.DMA,
            pltpu.SemaphoreType.DMA((2,)),
            pltpu.SemaphoreType.DMA((2, 2)),
        ],
        compiler_params=pltpu.CompilerParams(collective_id=0, has_side_effects=True),
        name="gather_factors",
    )(pay, tok, grad)


REDUCE = (((H, Y, X), 0, 144), ((X, H, Y), 144, 144), ((Y, X, H), 288, 128))


def add_into(dst, *terms):
    shape = dst.shape
    lead = shape[:-2]
    rows = shape[-2]
    count = math.prod(lead)

    def body(k, _):
        at = []
        for n in reversed(lead):
            at.append(k % n)
            k = k // n
        at = tuple(reversed(at))
        for r in range(0, rows, 16):
            here = at + (pl.ds(r, 16), slice(None))
            total = terms[0][here].astype(F32)
            for term in terms[1:]:
                total = total + term[here].astype(F32)
            dst[here] = total.astype(dst.dtype)
        return 0

    if count == 1:
        body(0, 0)
    else:
        lax.fori_loop(0, count, body, 0)


def reduce_kernel(scale, q_ref, out, *scratch):
    (send_sems, recv_sems), scratch = scratch[:2], scratch[2:]
    me = Place()
    me.greet()
    wire = Wire(send_sems, recv_sems)
    per_part = len(scratch) // 3

    def part(n):
        order, row0, rows = REDUCE[n]
        pool = list(scratch[n * per_part : (n + 1) * per_part])
        held = q_ref
        for stage, axis in enumerate(order):
            fixed = [me.at[a] if a in order[:stage] else None for a in range(3)]
            if stage:
                fixed = [0 if a in order[:stage] else None for a in range(3)]
            base = row0 if stage == 0 else 0
            staged = held if stage != 1 else pool.pop(0)
            nxt = pool.pop(0)
            first, second, third = pool.pop(0), pool.pop(0), pool.pop(0)
            dims = [a for a in range(3) if a != axis and fixed[a] is None]
            i = me.at[axis]

            def blk(ref, j, half=None, chunk=None, chunks=1):
                at0 = base if ref is held or ref is staged else 0
                return view(ref, fixed, axis, j, at0, rows, half, chunk, chunks)

            def send(j, half, dst, dst_j, device, extra=None, chunk=None, chunks=1):
                src = blk(staged, j, half, chunk, chunks)
                if extra is not None:
                    add_into(src, blk(held, j, half, chunk, chunks), extra)
                elif staged is not held:
                    add_into(src, blk(held, j, half, chunk, chunks))
                return wire(src, blk(dst, dst_j, half, chunk, chunks), device)

            if axis == H:
                l, s = me.l, me.s
                up, down, across = (i + s + 4) % 4, (i - s + 4) % 4, (i + 2) % 4
                chunks = 2 if stage == 0 else 1
                ids = range(chunks) if stage == 0 else (None,)
                a = [send(across, l, first, 0, me.pair, None, q, chunks) for q in ids]
                b = [send(down, 1 - l, second, 0, me.pair, None, q, chunks) for q in ids]
                yield
                c = []
                for k, q in enumerate(ids):
                    a[k].wait_recv()
                    c.append(send(across, 1 - l, first, 1, me.out, blk(first, 0, 1 - l, q, chunks), q, chunks))
                yield
                d = []
                for k, q in enumerate(ids):
                    b[k].wait_recv()
                    d.append(send(up, l, third, 0, me.out, blk(second, 0, l, q, chunks), q, chunks))
                yield
                e = []
                for k, q in enumerate(ids):
                    c[k].wait_recv()
                    e.append(send(down, l, second, 0, me.pair, blk(first, 1, l, q, chunks), q, chunks))
                yield
                f = []
                for k, q in enumerate(ids):
                    e[k].wait_recv()
                    f.append(send(up, 1 - l, third, 0, me.out, blk(second, 0, 1 - l, q, chunks), q, chunks))
                yield
                for k, q in enumerate(ids):
                    d[k].wait_recv()
                    add_into(blk(nxt, 0, 1 - l, q, chunks), blk(held, i, 1 - l, q, chunks), blk(third, 0, 1 - l, q, chunks))
                yield
                for k, q in enumerate(ids):
                    f[k].wait_recv()
                    add_into(blk(nxt, 0, l, q, chunks), blk(held, i, l, q, chunks), blk(third, 0, l, q, chunks))
            else:
                plus, minus = me.plus[axis], me.minus[axis]
                after, before, across = (i + 1) % 4, (i + 3) % 4, (i + 2) % 4
                a0 = send(across, 0, first, 0, plus)
                a1 = send(across, 1, first, 0, minus)
                b1 = send(after, 1, second, 0, plus)
                b0 = send(before, 0, third, 0, minus)
                yield
                a0.wait_recv()
                c0 = send(after, 0, second, 0, plus, blk(first, 0, 0))
                a1.wait_recv()
                c1 = send(before, 1, third, 0, minus, blk(first, 0, 1))
                yield
                b1.wait_recv()
                b0.wait_recv()
                yield
                c0.wait_recv()
                c1.wait_recv()
                for half in (0, 1):
                    add_into(blk(nxt, 0, half), blk(held, i, half), blk(second, 0, half), blk(third, 0, half))
            held = nxt
            yield
        other = pool.pop(0)
        swap = wire(held, other, me.pair)
        yield
        swap.wait_recv()
        place = out.at[me.c, pl.ds(row0, rows), :]
        place[...] = (held[0, 0, 0] + other[0, 0, 0]) * scale
        final = wire(place, place, me.sib)
        yield
        final.wait_recv()

    interleave([part(n) for n in range(3)])
    wire.finish()


def reduce_scratch():
    shapes = []
    for order, _, rows in REDUCE:
        dims = [SIDE] * 3
        for stage, axis in enumerate(order):
            if stage == 1:
                shapes.append(pltpu.VMEM(tuple(dims) + (rows, TB), BF))
            wire = BF if stage < 2 else F32
            dims[axis] = 1
            shapes.append(pltpu.VMEM(tuple(dims) + (rows, TB), F32))
            two = list(dims)
            two[axis] = 2
            shapes.append(pltpu.VMEM(tuple(two if axis == H else dims) + (rows, TB), wire))
            shapes += [pltpu.VMEM(tuple(dims) + (rows, TB), wire)] * 2
        shapes.append(pltpu.VMEM((1, 1, 1, rows, TB), F32))
    return shapes


def reduce(q, scale):
    return pl.pallas_call(
        lambda *refs: reduce_kernel(scale, *refs),
        out_shape=jax.ShapeDtypeStruct((2, QROWS, TB), F32),
        in_specs=[VMEM],
        out_specs=VMEM,
        scratch_shapes=[pltpu.SemaphoreType.DMA((80,)), pltpu.SemaphoreType.DMA((80,))] + reduce_scratch(),
        compiler_params=pltpu.CompilerParams(
            collective_id=1, has_side_effects=True, vmem_limit_bytes=40 * 1024 * 1024
        ),
        name="reduce_gradients",
    )(q)


def contract_rows(left, right):
    return lax.dot_general(left, right, (((0,), (0,)), ((), ())), preferred_element_type=F32)


def contract_cols(left, right):
    return lax.dot_general(left, right, (((1,), (1,)), ((), ())), preferred_element_type=F32)


def local(tokens, left_factor, right_factor, tile_values, tile_rows, tile_cols, grad_out):
    here = tokens.shape[0]
    grad_scale = 1.0 / math.sqrt(here * lax.axis_size("fsdp") * lax.axis_size("rep"))
    core = lax.axis_index("rep") % 2
    row_blocks, col_blocks = D // TB, FF // TB
    places = jnp.stack([tile_rows, tile_cols], 1).astype(BF)
    pay = jnp.concatenate(
        [
            left_factor.reshape(LEFT, 2, TB).transpose(1, 0, 2),
            right_factor.T.reshape(RIGHT, 2, TB).transpose(1, 0, 2),
            tile_values,
            jnp.broadcast_to(jnp.pad(places, ((0, 0), (0, TB - 2)))[:, None, :], (2, 16, TB)),
        ],
        1,
    )
    full, tok_s, grad_s = gather(pay, tokens, grad_out)
    full = full.reshape(2, 64, GROWS, TB)
    left_all = full[:, :, :LEFT].reshape(2, D, TB).transpose(1, 0, 2).reshape(D, R)
    right_all = full[:, :, LEFT : LEFT + RIGHT].reshape(2, FF, TB).transpose(1, 0, 2).reshape(FF, R)
    tiles_all = full[:, :, LEFT + RIGHT : QROWS].transpose(1, 0, 2, 3).reshape(128, TB, TB)
    index = full[:, :, QROWS, :2].astype(jnp.int32)
    rows_all = index[:, :, 0].T.reshape(128)
    cols_all = index[:, :, 1].T.reshape(128)

    both_tok = jnp.concatenate([tokens, tok_s], 0)
    both_grad = jnp.concatenate([grad_out, grad_s], 0)
    latent2 = jnp.dot(both_tok, left_all, preferred_element_type=F32).astype(BF)
    back2 = jnp.dot(both_grad, right_all, preferred_element_type=F32).astype(BF)
    latent, latent_grad = latent2[:here], back2[:here]

    token_tiles = jnp.take(tokens.reshape(here, row_blocks, TB), rows_all, axis=1)
    tile_prod = jnp.einsum("tkc,kcd->tkd", token_tiles, tiles_all, preferred_element_type=F32)
    sparse_out = jnp.zeros((here, col_blocks, TB), F32).at[:, cols_all].add(tile_prod).reshape(here, FF)
    out_rows = (contract_cols(latent, right_all) + sparse_out).astype(BF)
    grad_tiles = jnp.take(grad_out.reshape(here, col_blocks, TB), cols_all, axis=1)
    tile_back = jnp.einsum("tkd,kcd->tkc", grad_tiles, tiles_all, preferred_element_type=F32)
    sparse_back = jnp.zeros((here, row_blocks, TB), F32).at[:, rows_all].add(tile_back).reshape(here, D)
    input_grad = (contract_cols(latent_grad, left_all) + sparse_back).astype(BF)

    lat_h = lax.dynamic_slice_in_dim(latent2, core * TB, TB, 1)
    back_h = lax.dynamic_slice_in_dim(back2, core * TB, TB, 1)
    rows_h = lax.dynamic_index_in_dim(index[:, :, 0], core, 0, False)
    cols_h = lax.dynamic_index_in_dim(index[:, :, 1], core, 0, False)
    tok_h = jnp.take(both_tok.reshape(2 * here, row_blocks, TB), rows_h, axis=1)
    grad_h = jnp.take(both_grad.reshape(2 * here, col_blocks, TB), cols_h, axis=1)
    q = jnp.concatenate(
        [
            contract_rows(both_tok, back_h).astype(BF).reshape(64, LEFT, TB),
            contract_rows(both_grad, lat_h).astype(BF).reshape(64, RIGHT, TB),
            jnp.einsum("tkc,tkd->kcd", tok_h, grad_h, preferred_element_type=F32).astype(BF),
        ],
        1,
    ).reshape(SIDE, SIDE, SIDE, QROWS, TB)
    total = reduce(q, grad_scale)
    left_grad = total[:, :LEFT].transpose(1, 0, 2).reshape(LEFT, R)
    right_grad = total[:, LEFT : LEFT + RIGHT].transpose(0, 2, 1).reshape(R, RIGHT)
    return (out_rows, input_grad, left_grad, right_grad, total[:, LEFT + RIGHT :])


def solution(mesh):
    placed = (
        P(("rep", "fsdp"), None),
        P("fsdp", None),
        P(None, "fsdp"),
        P("fsdp", None, None),
        P("fsdp"),
        P("fsdp"),
        P(("rep", "fsdp"), None),
    )
    return jax.shard_map(
        local,
        mesh=mesh,
        in_specs=placed,
        out_specs=(
            P(("rep", "fsdp"), None),
            P(("rep", "fsdp"), None),
            P("fsdp", None),
            P(None, "fsdp"),
            P("fsdp", None, None),
        ),
        check_vma=False,
    )
```

time: 1290 us -> 312 us (0.24)
  waiting for transfers between devices: 1110 us -> 0 us
  Pallas kernels: 0 us -> 129 us
  local copies, waits for them, and re-layouts: 39 us -> 84.6 us
  blocking collectives: 22.3 us -> 0 us
  between operations: 14.9 us -> 0.96 us
    reduce_scatter x1 -> x0, waiting for transfers between devices: 398 us -> none  [local(): lax.psum_scatter(tile_flat, 'fsdp', scatter_dimension=0, tiled=True)]
    unnamed x8 -> x0, waiting for transfers between devices: 339 us -> none
    all_gather x4 -> x0, waiting for transfers between devices: 290 us -> none  [the longest x1 106 us: local(): right_all = lax.all_gather(right_factor, 'fsdp', axis=1, tiled=True)]
    pallas_call x0 -> x2, Pallas kernels: none -> 129 us  [the longest x1 70.2 us: gather(): pl.pallas_call(gather_kernel, out_shape=(jax.ShapeDtypeStruct((2, SIDE, S...]
    psum x1 -> x0, waiting for transfers between devices: 79.8 us -> none  [local(): lax.psum((left_shard, right_part, tile_shard), 'rep')]
    unnamed x1 -> x0, blocking collectives: 22.3 us -> none
    transpose x0 -> x8, local copies, waits for them, and re-layouts: none -> 18 us  [the longest x1 10.1 us: local(): full[:, :, LEFT:LEFT + RIGHT].reshape(2, FF, TB).transpose(1, 0, 2)]
  transfers between devices with their start and end apart: 8 -> 0, of which waited for: 7 -> 0; matrix products, arithmetic and copies ran while one was open for 10% -> 0% of each run, Pallas kernels for 0% -> 0%
where the time goes in v1:
time: 312 us; the launch traced here: 310 us
  Pallas kernels  129 us (41%)
  local copies, waits for them, and re-layouts  84.6 us (27%)
  matrix products  48.8 us (16%)
  other arithmetic  47.4 us (15%)
    pallas_call x1, Pallas kernels, gather(): pl.pallas_call(gather_kernel, out_shape=(jax.ShapeDtypeStruct((2, SIDE, S...  70.2 us
    pallas_call x1, Pallas kernels, reduce(): pl.pallas_call(lambda *refs: reduce_kernel(scale, *refs), out_shape=jax.S...  58.4 us
    scatter-add x1, other arithmetic, local(): jnp.zeros((here, col_blocks, TB), F32).at[:, cols_all].add(tile_prod)  26.3 us
    scatter-add x1, other arithmetic, local(): jnp.zeros((here, row_blocks, TB), F32).at[:, rows_all].add(tile_back)  17.1 us
    unnamed x23, local copies, waits for them, and re-layouts  15.7 us
    dot_general x2, matrix products, contract_cols(): lax.dot_general(left, right, (((1,), (1,)), ((), ())), preferred_element_...  11.3 us
    transpose x1, local copies, waits for them, and re-layouts, local(): full[:, :, LEFT:LEFT + RIGHT].reshape(2, FF, TB).transpose(1, 0, 2)  10.1 us
    dot_general x1, matrix products, local(): jnp.einsum('tkc,kcd->tkd', token_tiles, tiles_all, preferred_element_type...  8 us

profile of v1, /device:TPU:1, one launch (start us, length us, event | category | flops | bytes accessed | tf_op | source)
XLA Modules:
  0.0 310.4 jit_solution(17654440910669784292)
XLA Ops:
  2.3 1.5 pad_maximum_fusion.1.pay
  3.9 70.2 %gather_factors.1 = (bf16[2,4,4,4,432,128]{5,4,3,2,1,0:T(8,128)(2,1)}, bf16[128,4096]{1,0:T(8,128)(2,1)}, bf16[128,14336]{1,0:T(8,128)(2,1)}) custom-call(bf16[2,432,128]{2,1,0:T(8,128)(2,1)} %pad_maximum_fusion.1.pay, bf16[128,4096]{1,0:T(8,128)(2,1)} %tok.1, bf16[128,14336]{1,0:T(8,128)(2,1)} %grad.1), custom_call_target="tpu_custom_call" | custom-call | tf_op jit(solution)/shard_map/gather_factors/pallas_call | solution.py:231
  75.5 2.4 constant_dynamic-update-slice_fusion.3
  78.2 3.0 copy-done.2
  81.2 5.0 %copy_bitcast_fusion = bf16[256,112,128]{2,0,1:T(8,128)(2,1)} fusion(bf16[256,14336]{1,0:T(8,128)(2,1)S(1)} %constant_dynamic-update-slice_fusion.2), kind=kLoop, calls=%fused_computation.9 | loop fusion | bytes 14680064 | tf_op jit(solution)/shard_map/reshape | solution.py:470
  86.2 6.2 %gather_fusion.3 = bf16[64,256,128]{2,1,0:T(8,128)(2,1)} fusion(bf16[256,112,128]{2,0,1:T(8,128)(2,1)} %copy_bitcast_fusion, s32[1024]{0:T(1024)S(1)} %pad_clamp_fusion), kind=kCustom, calls=%fused_computation.3 | custom fusion | bytes 8388864 | tf_op jit(solution)/shard_map/jit(_take)/gather | solution.py:470
  92.7 1.3 constant_dynamic-update-slice_fusion
  94.0 1.9 copy_bitcast_fusion.1
  95.9 4.6 %gather_fusion.2 = bf16[64,256,128]{2,1,0:T(8,128)(2,1)} fusion(bf16[256,32,128]{2,0,1:T(8,128)(2,1)} %copy_bitcast_fusion.1, s32[1024]{0:T(1024)S(1)} %pad_clamp_fusion.1), kind=kCustom, calls=%fused_computation.2 | custom fusion | bytes 8388864 | tf_op jit(solution)/shard_map/jit(_take)/gather | solution.py:469
  100.5 6.5 %fusion.20 = bf16[64,128,128]{2,1,0:T(8,128)(2,1)} fusion(bf16[64,256,128]{2,1,0:T(8,128)(2,1)} %gather_fusion.3, pred[64]{0:T(512)(128)(4,1)S(1)} %compare_and_fusion, bf16[64,256,128]{2,1,0:T(8,128)(2,1)} %gather_fusion.2, pred[64]{0:T(512)(128)(4,1)S(1)} %compare_and_fusion.1), kind=kOutput, calls=%fused_computation.34 | convolution fusion | flops 542113792 | bytes 10485888 | tf_op jit(solution)/shard_map/tkc,tkd->kcd/dot_general | solution.py:475
  107.1 6.5 %slice.56 = bf16[2,64,224,128]{3,2,1,0:T(8,128)(2,1)} slice(bf16[2,64,432,128]{3,2,1,0:T(8,128)(2,1)} %bitcast.117), slice={[0:2], [0:64], [64:288], [0:128]} | slice | bytes 14680064 | tf_op jit(solution)/shard_map/slice | solution.py:444
  113.6 10.1 %copy.65 = bf16[14336,2,128]{0,2,1:T(8,128)(2,1)} copy(bf16[14336,2,128]{2,0,1:T(8,128)(2,1)} %bitcast.113) | data formatting | bytes 14680064 | tf_op jit(solution)/shard_map/transpose | solution.py:444
  123.7 7.3 %convolution_convert_fusion.2 = bf16[256,256]{1,0:T(8,128)(2,1)S(1)} fusion(bf16[256,14336]{1,0:T(8,128)(2,1)} %copy-done.2, bf16[14336,256]{0,1:T(8,128)(2,1)} %bitcast.111), kind=kOutput, calls=%fused_computation.35 | convolution fusion | flops 1879113728 | bytes 14811136 | tf_op jit(solution)/shard_map/dot_general | solution.py:453
  131.0 1.7 convolution_convert_fusion.1
  132.7 3.1 slice.54
  135.8 4.1 %copy.64 = bf16[4096,2,128]{0,2,1:T(8,128)(2,1)} copy(bf16[4096,2,128]{2,0,1:T(8,128)(2,1)} %bitcast.121) | data formatting | bytes 4194304 | tf_op jit(solution)/shard_map/transpose | solution.py:443
  139.9 2.3 convolution_convert_fusion.3
  142.3 5.4 %convolution_convert_fusion = bf16[14336,128]{1,0:T(8,128)(2,1)S(1)} fusion(bf16[256,14336]{1,0:T(8,128)(2,1)} %copy-done.2, bf16[256,256]{1,0:T(8,128)(2,1)S(1)} %convolution_convert_fusion.3, s32[]{:T(128)S(6)} %select_n.103), kind=kOutput, calls=%fused_computation.8 | convolution fusion | flops 941359104 | bytes 11075588 | tf_op jit(solution)/shard_map/dot_general | solution.py:419
  148.3 58.4 %reduce_gradients.1 = f32[2,416,128]{2,1,0:T(8,128)S(1)} custom-call(bf16[4,4,4,416,128]{4,3,2,1,0:T(8,128)(2,1)S(1)} %pad_maximum_fusion.refs_0_), custom_call_target="tpu_custom_call" | custom-call | tf_op jit(solution)/shard_map/reduce_gradients/pallas_call | solution.py:405
  209.0 6.1 %copy.74 = bf16[128,14336]{0,1:T(8,128)(2,1)} copy(bf16[128,14336]{1,0:T(8,128)(2,1)} %grad.1) | data formatting | bytes 7340032 | tf_op args[6]
  215.0 5.9 %copy.75 = bf16[128,112,128]{2,0,1:T(8,128)(2,1)} copy(bf16[128,112,128]{0,2,1:T(8,128)(2,1)} %bitcast.115) | data formatting | bytes 7340032 | tf_op jit(solution)/shard_map/reshape | solution.py:460
  220.9 5.1 %gather_fusion.1 = bf16[128,128,128]{2,1,0:T(8,128)(2,1)} fusion(bf16[128,112,128]{2,0,1:T(8,128)(2,1)} %copy.75, s32[1024]{0:T(1024)S(1)} %pad_clamp_fusion.2), kind=kCustom, calls=%fused_computation.1 | custom fusion | bytes 8389120 | tf_op jit(solution)/shard_map/jit(_take)/gather | solution.py:460
  226.2 2.5 slice_bitcast_fusion
  229.1 3.4 %copy-done.4 = bf16[128,128,128]{2,1,0:T(8,128)(2,1)S(1)} copy-done((bf16[128,128,128]{2,1,0:T(8,128)(2,1)S(1)}, bf16[128,128,128]{2,1,0:T(8,128)(2,1)}, u32[]{:S(2)}) %copy-start.4) | copy-done | bytes 4194328
  232.4 6.3 %fusion.5 = f32[128,128,128]{2,1,0:T(8,128)} fusion(bf16[128,128,128]{2,1,0:T(8,128)(2,1)S(1)} %bitcast.109, bf16[128,128,128]{2,1,0:T(8,128)(2,1)S(1)} %copy-done.4, pred[128]{0:T(512)(128)(4,1)S(1)} %compare_and_fusion.2), kind=kOutput, calls=%fused_computation.18 | convolution fusion | flops 538968064 | bytes 16777344 | tf_op jit(solution)/shard_map/tkd,kcd->tkc/dot_general | solution.py:461
  239.2 17.1 %scatter_fusion.1 = f32[128,32,128]{2,0,1:T(8,128)S(1)} fusion(f32[128,32,128]{2,0,1:T(8,128)S(1)} %broadcast_in_dim.54, s32[128]{0:T(128)S(1)} %fusion.32, f32[128,128,128]{2,1,0:T(8,128)} %fusion.5), kind=kCustom, calls=%fused_computation.5 | custom fusion | flops 2097152 | bytes 25166336 | tf_op jit(solution)/shard_map/scatter-add | solution.py:462
  256.3 3.0 fusion.1
  260.7 3.1 gather_fusion
  263.9 8.0 %fusion.7 = f32[128,128,128]{2,1,0:T(8,128)} fusion(bf16[128,128,128]{2,1,0:T(8,128)(2,1)} %bitcast.110, bf16[128,128,128]{2,1,0:T(8,128)(2,1)} %gather_fusion, pred[128]{0:T(512)(128)(4,1)S(1)} %compare_and_fusion.3), kind=kOutput, calls=%fused_computation.20 | convolution fusion | flops 538968064 | bytes 16777344 | tf_op jit(solution)/shard_map/tkc,kcd->tkd/dot_general | solution.py:457
  271.9 3.9 %broadcast_in_dim.51 = f32[128,112,128]{2,0,1:T(8,128)} broadcast(f32[]{:T(128)} %constant.80.clone.1), dimensions={} | broadcast | bytes 7340036 | tf_op jit(solution)/shard_map/broadcast_in_dim | solution.py:458
  275.8 26.3 %scatter_fusion = f32[128,112,128]{2,0,1:T(8,128)} fusion(f32[128,112,128]{2,0,1:T(8,128)} %broadcast_in_dim.51, s32[128]{0:T(128)S(1)} %fusion.31, f32[128,128,128]{2,1,0:T(8,128)} %fusion.7), kind=kCustom, calls=%fused_computation.4 | custom fusion | flops 2097152 | bytes 25166336 | tf_op jit(solution)/shard_map/scatter-add | solution.py:458
  302.1 8.3 %fusion = bf16[128,14336]{1,0:T(8,128)(2,1)} fusion(bf16[14336,256]{0,1:T(8,128)(2,1)} %bitcast.112, bf16[256,256]{1,0:T(8,128)(2,1)S(1)} %convolution_convert_fusion.3, f32[128,112,128]{2,0,1:T(8,128)} %scatter_fusion), kind=kOutput, calls=%fused_computation.7 | convolution fusion | flops 943194112 | bytes 18415616 | tf_op jit(solution)/shard_map/dot_general | solution.py:423
  (55 shorter events, 8.9 us)
Async XLA Ops:
  0.6 0.9 copy-start
  74.0 3.9 %copy-start.7 = (bf16[128,14336]{1,0:T(8,128)(2,1)S(1)}, bf16[128,14336]{1,0:T(8,128)(2,1)}, u32[]{:S(2)}) copy-start(bf16[128,14336]{1,0:T(8,128)(2,1)} %get-tuple-element.10) | copy-start | bytes 11010052
  78.2 3.0 copy-start.2
  86.2 6.4 %copy-start.5 = (bf16[128,4096]{1,0:T(8,128)(2,1)S(1)}, bf16[128,4096]{1,0:T(8,128)(2,1)}, u32[]{:S(2)}) copy-start(bf16[128,4096]{1,0:T(8,128)(2,1)} %tok.1) | copy-start | bytes 3145732
  142.3 5.4 %copy-start.6 = (bf16[4096,128]{1,0:T(8,128)(2,1)S(1)}, bf16[4096,128]{1,0:T(8,128)(2,1)}, u32[]{:S(2)}) copy-start(bf16[4096,128]{1,0:T(8,128)(2,1)} %convolution_convert_fusion.1) | copy-start | bytes 3145732
  142.3 5.4 %copy-start.8 = (bf16[64,128,128]{2,1,0:T(8,128)(2,1)S(1)}, bf16[64,128,128]{2,1,0:T(8,128)(2,1)}, u32[]{:S(2)}) copy-start(bf16[64,128,128]{2,1,0:T(8,128)(2,1)} %fusion.20) | copy-start | bytes 6291460
  228.7 3.7 %copy-start.4 = (bf16[128,128,128]{2,1,0:T(8,128)(2,1)S(1)}, bf16[128,128,128]{2,1,0:T(8,128)(2,1)}, u32[]{:S(2)}) copy-start(bf16[128,128,128]{2,1,0:T(8,128)(2,1)} %gather_fusion.1) | copy-start | bytes 12582916
  229.1 9.7 %copy-start.3 = (bf16[64,2,128,128]{3,2,1,0:T(8,128)(2,1)}, bf16[64,2,128,128]{3,2,1,0:T(8,128)(2,1)S(1)}, u32[]{:S(2)}) copy-start(bf16[64,2,128,128]{3,2,1,0:T(8,128)(2,1)S(1)} %copy.71) | copy-start | bytes 12582916
  302.1 8.3 %copy-start.1 = (bf16[256,224]{0,1:T(8,128)(2,1)S(1)}, bf16[256,224]{0,1:T(8,128)(2,1)}, u32[]{:S(2)}) copy-start(bf16[256,224]{0,1:T(8,128)(2,1)} %param.9) | copy-start | bytes 344068

commit v2 on v1

--- a/solution.py
+++ b/solution.py
@@ -35,6 +35,9 @@
         self.out = self.dev(low=1 - self.l, step=(H, self.s))
         self.plus = {a: self.dev(step=(a, 1)) for a in (Y, X)}
         self.minus = {a: self.dev(step=(a, 3)) for a in (Y, X)}
+        self.direct = {a: [self.dev(step=(a, k)) for k in (1, 3, 2)] for a in (Y, X)}
+        self.direct[H] = [self.out, self.dev(step=(H, self.s)), self.dev(low=1 - self.l, step=(H, 2))]
+        self.behind = self.dev(step=(H, -self.s))
 
     def dev(self, core=None, low=None, step=None):
         core = self.c if core is None else core
@@ -46,7 +49,7 @@
 
     def greet(self):
         barrier = pltpu.get_barrier_semaphore()
-        near = [self.sib, self.pair, self.out] + [d[a] for d in (self.plus, self.minus) for a in (Y, X)]
+        near = [self.sib, self.pair, self.behind] + [d for a in (Y, H, X) for d in self.direct[a]]
         for device in near:
             pl.semaphore_signal(barrier, inc=1, device_id=device, device_id_type=MESH)
         pl.semaphore_wait(barrier, len(near))
@@ -74,16 +77,6 @@
     def finish(self):
         for copy in self.started:
             copy.wait_send()
-
-
-def interleave(parts):
-    parts = list(parts)
-    while parts:
-        for part in list(parts):
-            try:
-                next(part)
-            except StopIteration:
-                parts.remove(part)
 
 
 def view(ref, fixed, axis, j, row0, rows, half=None, chunk=None, chunks=1):
@@ -106,7 +99,75 @@
     return ref.at[sel[0], sel[1], sel[2], pl.ds(r0, n), :]
 
 
-GATHER = (((X, Y, H), 0, 144), ((Y, H, X), 144, 160), ((H, X, Y), 304, 128))
+GATHER = (((X, Y, H), 0, 80), ((Y, H, X), 80, 176), ((H, X, Y), 256, 176))
+
+
+def run_all(active):
+    while active:
+        for run in list(active):
+            try:
+                next(run)
+            except StopIteration:
+                active.remove(run)
+
+
+def spread(me, axis, send, got, ready):
+    i = me.at[axis]
+    across = (i + 2) % 4
+    if axis == H:
+        l, s = me.l, me.s
+        up, down = (i + s + 4) % 4, (i - s + 4) % 4
+        a, b = send(i, 1 - l, me.out), send(i, l, me.out)
+        yield
+        a.wait_recv()
+        f = send(up, l, me.pair)
+        got(up, l)
+        yield
+        b.wait_recv()
+        e = send(up, 1 - l, me.pair)
+        got(up, 1 - l)
+        ready(up)
+        yield
+        f.wait_recv()
+        g = send(down, 1 - l, me.out)
+        got(down, 1 - l)
+        yield
+        e.wait_recv()
+        got(down, l)
+        ready(down)
+        yield
+        g.wait_recv()
+        w = send(across, l, me.pair)
+        got(across, l)
+        yield
+        w.wait_recv()
+        got(across, 1 - l)
+        ready(across)
+    else:
+        plus, minus = me.plus[axis], me.minus[axis]
+        after, before = (i + 1) % 4, (i + 3) % 4
+        a0, b1 = send(i, 0, plus), send(i, 1, minus)
+        a1, b0 = send(i, 1, plus), send(i, 0, minus)
+        yield
+        a0.wait_recv()
+        c0 = send(before, 0, plus)
+        got(before, 0)
+        b1.wait_recv()
+        c1 = send(after, 1, minus)
+        got(after, 1)
+        yield
+        a1.wait_recv()
+        got(before, 1)
+        ready(before)
+        b0.wait_recv()
+        got(after, 0)
+        ready(after)
+        yield
+        c0.wait_recv()
+        got(across, 0)
+        c1.wait_recv()
+        got(across, 1)
+        ready(across)
 
 
 def gather_kernel(pay, tok, grad, full, tok_s, grad_s, send_sems, recv_sems, local_sem, side_sems, wide_sems):
@@ -115,7 +176,9 @@
     own = pltpu.make_async_copy(pay.at[me.c], mine.at[me.at[0], me.at[1], me.at[2]], local_sem)
     own.start()
     me.greet()
+    own.wait()
     wire = Wire(send_sems, recv_sems)
+    active = []
 
     def to_sibling(src, dst, pair):
         return pltpu.make_async_remote_copy(
@@ -128,98 +191,54 @@
         )
 
     def part(order, row0, rows):
-        for stage, axis in enumerate(order):
-            fixed = [None if a in order[:stage] else me.at[a] for a in range(3)]
-            last = stage == 2
-
-            def blk(j, half=None, chunk=None, chunks=1):
-                return view(mine, fixed, axis, j, row0, rows, half, chunk, chunks)
-
-            def src(j, half, chunk=None, chunks=1):
-                if stage:
-                    return blk(j, half, chunk, chunks)
-                return view(pay.at[pl.ds(me.c, 1)].reshape(1, 1, 1, GROWS, TB), [0, 0, 0], axis, 0, row0, rows, half)
-
-            def got(ref):
-                if last:
-                    to_sibling(ref, ref, side_sems).start()
-
-            def send(j, half, device, chunk=None, chunks=1, first=False):
-                ref = blk(j, half, chunk, chunks)
+        one, two, three = order
+
+        def piece(at, half=None):
+            sel = [at.get(a, slice(None)) for a in range(3)]
+            if half is not None:
+                sel[one] = pl.ds(half * 2, 2)
+            return mine.at[sel[0], sel[1], sel[2], pl.ds(row0, rows), :]
+
+        def last(j2):
+            def send(j, half, device):
+                ref = piece({two: j2, three: j}, half)
                 return wire(ref, ref, device)
 
-            i = me.at[axis]
-            if last:
-                got(blk(i))
-            if axis == H:
-                l, s = me.l, me.s
-                up, down, across = (i + s + 4) % 4, (i - s + 4) % 4, (i + 2) % 4
-                chunks = 2 if last else 1
-                ids = range(chunks) if last else (None,)
-                a = [send(i, 1 - l, me.out, q, chunks) for q in ids]
-                b = [send(i, l, me.out, q, chunks) for q in ids]
-                yield
-                f = []
-                for k, q in enumerate(ids):
-                    a[k].wait_recv()
-                    f.append(send(up, l, me.pair, q, chunks))
-                    got(blk(up, l, q, chunks))
-                yield
-                e = []
-                for k, q in enumerate(ids):
-                    b[k].wait_recv()
-                    e.append(send(up, 1 - l, me.pair, q, chunks))
-                    got(blk(up, 1 - l, q, chunks))
-                yield
-                g = []
-                for k, q in enumerate(ids):
-                    f[k].wait_recv()
-                    g.append(send(down, 1 - l, me.out, q, chunks))
-                    got(blk(down, 1 - l, q, chunks))
-                yield
-                for k, q in enumerate(ids):
-                    e[k].wait_recv()
-                    got(blk(down, l, q, chunks))
-                w = []
-                for k, q in enumerate(ids):
-                    g[k].wait_recv()
-                    w.append(send(across, l, me.pair, q, chunks))
-                    got(blk(across, l, q, chunks))
-                yield
-                for k, q in enumerate(ids):
-                    w[k].wait_recv()
-                    got(blk(across, 1 - l, q, chunks))
-            else:
-                plus, minus = me.plus[axis], me.minus[axis]
-                after, before, across = (i + 1) % 4, (i + 3) % 4, (i + 2) % 4
-                a0, b1 = send(i, 0, plus), send(i, 1, minus)
-                a1, b0 = send(i, 1, plus), send(i, 0, minus)
-                yield
-                a0.wait_recv()
-                c0 = send(before, 0, plus)
-                got(blk(before, 0))
-                b1.wait_recv()
-                c1 = send(after, 1, minus)
-                got(blk(after, 1))
-                yield
-                a1.wait_recv()
-                got(blk(before, 1))
-                b0.wait_recv()
-                got(blk(after, 0))
-                yield
-                c0.wait_recv()
-                got(blk(across, 0))
-                c1.wait_recv()
-                got(blk(across, 1))
-
-    own.wait()
-    runs = [part(*p) for p in GATHER]
-    for run in runs:
+            def got(j, half):
+                ref = piece({two: j2, three: j}, half)
+                to_sibling(ref, ref, side_sems).start()
+
+            ref = piece({two: j2, three: me.at[three]})
+            to_sibling(ref, ref, side_sems).start()
+            return spread(me, three, send, got, lambda j: None)
+
+        def start_last(j2):
+            run = last(j2)
+            next(run)
+            active.append(run)
+
+        def send(j, half, device):
+            ref = piece({two: j, three: me.at[three]}, half)
+            return wire(ref, ref, device)
+
+        seed = piece({a: me.at[a] for a in range(3)})
+        seeds = [wire(seed, seed, device) for device in me.direct[one]]
+        yield
+        for copy in seeds:
+            copy.wait_recv()
+        run = spread(me, two, send, lambda j, half: None, start_last)
+        next(run)
+        start_last(me.at[two])
+        active.append(run)
+
+    for p in GATHER:
+        active.append(part(*p))
+    for run in active:
         next(run)
     swaps = [to_sibling(tok, tok_s, wide_sems.at[0]), to_sibling(grad, grad_s, wide_sems.at[1])]
     for swap in swaps:
         swap.start()
-    interleave(runs)
+    run_all(active)
     wire.finish()
     for swap in swaps:
         swap.wait()
@@ -238,8 +257,8 @@
         in_specs=[ANY] * 3,
         out_specs=(ANY,) * 3,
         scratch_shapes=[
-            pltpu.SemaphoreType.DMA((80,)),
-            pltpu.SemaphoreType.DMA((80,)),
+            pltpu.SemaphoreType.DMA((120,)),
+            pltpu.SemaphoreType.DMA((120,)),
             pltpu.SemaphoreType.DMA,
             pltpu.SemaphoreType.DMA((2,)),
             pltpu.SemaphoreType.DMA((2, 2)),
@@ -278,10 +297,8 @@
         lax.fori_loop(0, count, body, 0)
 
 
-def reduce_kernel(scale, q_ref, out, *scratch):
+def reduce_parts(me, scale, q_ref, out, scratch):
     (send_sems, recv_sems), scratch = scratch[:2], scratch[2:]
-    me = Place()
-    me.greet()
     wire = Wire(send_sems, recv_sems)
     per_part = len(scratch) // 3
 
@@ -294,7 +311,7 @@
             if stage:
                 fixed = [0 if a in order[:stage] else None for a in range(3)]
             base = row0 if stage == 0 else 0
-            staged = held if stage != 1 else pool.pop(0)
+            staged = held
             nxt = pool.pop(0)
             first, second, third = pool.pop(0), pool.pop(0), pool.pop(0)
             dims = [a for a in range(3) if a != axis and fixed[a] is None]
@@ -308,8 +325,6 @@
                 src = blk(staged, j, half, chunk, chunks)
                 if extra is not None:
                     add_into(src, blk(held, j, half, chunk, chunks), extra)
-                elif staged is not held:
-                    add_into(src, blk(held, j, half, chunk, chunks))
                 return wire(src, blk(dst, dst_j, half, chunk, chunks), device)
 
             if axis == H:
@@ -379,8 +394,7 @@
         yield
         final.wait_recv()
 
-    interleave([part(n) for n in range(3)])
-    wire.finish()
+    return [part(n) for n in range(3)] + [wire.finish]
 
 
 def reduce_scratch():
@@ -388,9 +402,7 @@
     for order, _, rows in REDUCE:
         dims = [SIDE] * 3
         for stage, axis in enumerate(order):
-            if stage == 1:
-                shapes.append(pltpu.VMEM(tuple(dims) + (rows, TB), BF))
-            wire = BF if stage < 2 else F32
+            wire = BF if stage < 1 else F32
             dims[axis] = 1
             shapes.append(pltpu.VMEM(tuple(dims) + (rows, TB), F32))
             two = list(dims)
@@ -401,18 +413,24 @@
     return shapes
 
 
-def reduce(q, scale):
-    return pl.pallas_call(
-        lambda *refs: reduce_kernel(scale, *refs),
-        out_shape=jax.ShapeDtypeStruct((2, QROWS, TB), F32),
-        in_specs=[VMEM],
-        out_specs=VMEM,
-        scratch_shapes=[pltpu.SemaphoreType.DMA((80,)), pltpu.SemaphoreType.DMA((80,))] + reduce_scratch(),
-        compiler_params=pltpu.CompilerParams(
-            collective_id=1, has_side_effects=True, vmem_limit_bytes=40 * 1024 * 1024
-        ),
-        name="reduce_gradients",
-    )(q)
+def run_with(active, work):
+    while active:
+        for run in list(active):
+            try:
+                next(run)
+            except StopIteration:
+                active.remove(run)
+        next(work, None)
+    for _ in work:
+        pass
+
+
+CHUNKS = 8
+PER = 64 // CHUNKS
+WIDE = PER * RIGHT
+SLICES = 4
+EMPTY = 128
+PIECE = 2048
 
 
 def contract_rows(left, right):
@@ -423,11 +441,189 @@
     return lax.dot_general(left, right, (((1,), (1,)), ((), ())), preferred_element_type=F32)
 
 
+def dot(left, right):
+    return jnp.dot(left, right, preferred_element_type=F32)
+
+
+def wide(ref, first, count, rows=None):
+    return jnp.concatenate([ref[n] if rows is None else ref[n, :rows] for n in range(first, first + count)], 1)
+
+
+def load(src, dst, sem):
+    copy = pltpu.make_async_copy(src, dst, sem)
+    copy.start()
+    return copy
+
+
+def products_kernel(scale, places, order, same, full, tok, tok_s, grad, grad_s, total, out, back_out, *scratch):
+    (q, left, right, tiles, tok2, grad2, run, latent, latent_o, back_c, back_o, stage) = scratch[:12]
+    left_sems, right_sems, tile_sem, stage_sems = scratch[12:16]
+    me = Place()
+    c, o = me.c, 1 - me.c
+    here = tok.shape[0]
+    pieces = [(tok, tok_s, tok2, n) for n in range(D // PIECE)] + [(grad, grad_s, grad2, n) for n in range(FF // PIECE)]
+
+    def fetch(k):
+        own, other, _, n = pieces[k]
+        span = pl.ds(n * PIECE, PIECE)
+        return [
+            load(own.at[:, span], stage.at[k % 3, pl.ds(0, here)], stage_sems.at[0, k % 3]),
+            load(other.at[:, span], stage.at[k % 3, pl.ds(here, here)], stage_sems.at[1, k % 3]),
+        ]
+
+    coming = [fetch(k) for k in range(3)]
+    left_in, right_in = [], []
+    for k, half in enumerate((c, o)):
+        left_in.append(load(full.at[half, :, pl.ds(0, LEFT), :], left.at[k], left_sems.at[k]))
+        right_in.append(load(full.at[half, :, pl.ds(LEFT, RIGHT), :], right.at[k], right_sems.at[k]))
+    tiles_in = load(full.at[:, :, pl.ds(LEFT + RIGHT, TB), :], tiles, tile_sem)
+    me.greet()
+    runs = reduce_parts(me, scale, q, total, scratch[16:])
+
+    def tile_part(g, _):
+        for u in range(8):
+            t = 2 * (g * 8 + u) + c
+            part = contract_rows(tok2[places[0, t]], grad2[places[1, t]])
+            q[g // 2, (g % 2) * 2 + u // 4, u % 4, LEFT + RIGHT :, :] = part.astype(BF)
+        return 0
+
+    for k, (_, _, held, n) in enumerate(pieces):
+        for copy in coming[k]:
+            copy.wait()
+        for b in range(PIECE // TB):
+            held[n * (PIECE // TB) + b] = stage[k % 3, :, b * TB : (b + 1) * TB]
+        if k + 3 < len(pieces):
+            coming.append(fetch(k + 3))
+    lax.fori_loop(0, 8, tile_part, 0)
+    next(runs[2])
+
+    left_in[0].wait()
+    latent[...] = dot(wide(tok2, 0, D // TB), left[0].reshape(D, TB)).astype(BF)
+    right_in[0].wait()
+    back = jnp.zeros((2 * here, TB), F32)
+    for j in range(CHUNKS):
+        part = wide(grad2, j * WIDE // TB, WIDE // TB)
+        back = back + dot(part, right[0, j * PER : (j + 1) * PER].reshape(WIDE, TB))
+        q[j // 2, (j % 2) * 2 : (j % 2) * 2 + 2, :, LEFT : LEFT + RIGHT, :] = (
+            contract_rows(part, latent[...]).astype(BF).reshape(2, 4, RIGHT, TB)
+        )
+    next(runs[1])
+    back_c[...] = back.astype(BF)
+    for j in range(4):
+        part = contract_rows(wide(tok2, j * 8, 8), back_c[...])
+        q[j, :, :, :LEFT, :] = part.astype(BF).reshape(4, 4, LEFT, TB)
+    next(runs[0])
+
+    def running_sums(which, product, g0):
+        def body(g, held):
+            parts = [product(g * 8 + u) for u in range(8)]
+            for u in range(8):
+                t = g * 8 + u
+                held = held * same[which, t] + parts[u]
+                run[t] = held
+            return held
+
+        before = jnp.zeros((here, TB), F32) if g0 == 0 else run[g0 * 8 - 1]
+        lax.fori_loop(g0, g0 + 16 // SLICES, body, before)
+
+    def ahead(t):
+        return dot(tok2[order[0, 0, t], :here], tiles[order[0, 1, t], order[0, 2, t]])
+
+    def behind(t):
+        return contract_cols(grad2[order[1, 0, t], :here], tiles[order[1, 1, t], order[1, 2, t]])
+
+    def work():
+        left_in[1].wait()
+        latent_o[...] = dot(wide(tok2, 0, D // TB, here), left[1].reshape(D, TB)).astype(BF)
+        tiles_in.wait()
+        run[EMPTY] = jnp.zeros((here, TB), F32)
+        for n in range(SLICES):
+            running_sums(0, ahead, n * 16 // SLICES)
+            yield
+        right_in[1].wait()
+        back_o[...] = jnp.zeros((here, TB), F32)
+        for j in range(CHUNKS):
+            rights = [right[k, j * PER : (j + 1) * PER].reshape(WIDE, TB) for k in (0, 1)]
+            back_o[...] += dot(wide(grad2, j * WIDE // TB, WIDE // TB, here), rights[1])
+            dense = contract_cols(latent[:here], rights[0]) + contract_cols(latent_o[...], rights[1])
+            for b in range(WIDE // TB):
+                n = j * (WIDE // TB) + b
+                out[:, n * TB : (n + 1) * TB] = (dense[:, b * TB : (b + 1) * TB] + run[order[0, 3, n]]).astype(BF)
+            yield
+        for n in range(SLICES):
+            running_sums(1, behind, n * 16 // SLICES)
+            yield
+        back_h = back_o[...].astype(BF)
+        for j in range(4):
+            lefts = [left[k, j * 16 : (j + 1) * 16].reshape(1024, TB) for k in (0, 1)]
+            dense = contract_cols(back_c[:here], lefts[0]) + contract_cols(back_h, lefts[1])
+            for b in range(8):
+                n = j * 8 + b
+                back_out[:, n * TB : (n + 1) * TB] = (dense[:, b * TB : (b + 1) * TB] + run[order[1, 3, n]]).astype(BF)
+            if j % 2:
+                yield
+
+    run_with(list(runs[:3]), work())
+    runs[3]()
+
+
+def products(places, order, same, full, tok, tok_s, grad, grad_s, scale):
+    here = tok.shape[0]
+    return pl.pallas_call(
+        lambda *refs: products_kernel(scale, *refs),
+        out_shape=(
+            jax.ShapeDtypeStruct((2, QROWS, TB), F32),
+            jax.ShapeDtypeStruct((here, FF), BF),
+            jax.ShapeDtypeStruct((here, D), BF),
+        ),
+        in_specs=[pl.BlockSpec(memory_space=pltpu.SMEM)] * 3 + [ANY] * 5,
+        out_specs=(VMEM,) * 3,
+        scratch_shapes=[
+            pltpu.VMEM((SIDE, SIDE, SIDE, QROWS, TB), BF),
+            pltpu.VMEM((2, 64, LEFT, TB), BF),
+            pltpu.VMEM((2, 64, RIGHT, TB), BF),
+            pltpu.VMEM((2, 64, TB, TB), BF),
+            pltpu.VMEM((D // TB, 2 * here, TB), BF),
+            pltpu.VMEM((FF // TB, 2 * here, TB), BF),
+            pltpu.VMEM((EMPTY + 1, here, TB), F32),
+            pltpu.VMEM((2 * here, TB), BF),
+            pltpu.VMEM((here, TB), BF),
+            pltpu.VMEM((2 * here, TB), BF),
+            pltpu.VMEM((here, TB), F32),
+            pltpu.VMEM((3, 2 * here, PIECE), BF),
+            pltpu.SemaphoreType.DMA((2,)),
+            pltpu.SemaphoreType.DMA((2,)),
+            pltpu.SemaphoreType.DMA,
+            pltpu.SemaphoreType.DMA((2, 3)),
+            pltpu.SemaphoreType.DMA((80,)),
+            pltpu.SemaphoreType.DMA((80,)),
+        ]
+        + reduce_scratch(),
+        compiler_params=pltpu.CompilerParams(
+            collective_id=1, has_side_effects=True, vmem_limit_bytes=62 * 1024 * 1024
+        ),
+        name="products_and_reduction",
+    )(places, order, same, full, tok, tok_s, grad, grad_s)
+
+
+def sorted_tiles(places):
+    ids = jnp.arange(128, dtype=jnp.int32)
+    found, joins = [], []
+    for key, other in ((places[1], places[0]), (places[0], places[1])):
+        unique = key * 128 + ids
+        rank = jnp.sum((unique[None, :] < unique[:, None]).astype(jnp.int32), 1)
+        at = rank[None, :] == ids[:, None]
+        pick = lambda v: jnp.sum(jnp.where(at, v[None, :], 0), 1)
+        by = pick(key)
+        joins.append(jnp.concatenate([jnp.zeros((1,), F32), (by[1:] == by[:-1]).astype(F32)]))
+        upto = jnp.sum((key[None, :] <= ids[:, None]).astype(jnp.int32), 1)
+        present = jnp.any(key[None, :] == ids[:, None], 1)
+        found.append(jnp.stack([pick(other), pick(ids % 2), pick(ids // 2), jnp.where(present, upto - 1, EMPTY)]))
+    return jnp.stack(found), jnp.stack(joins)
+
+
 def local(tokens, left_factor, right_factor, tile_values, tile_rows, tile_cols, grad_out):
-    here = tokens.shape[0]
-    grad_scale = 1.0 / math.sqrt(here * lax.axis_size("fsdp") * lax.axis_size("rep"))
-    core = lax.axis_index("rep") % 2
-    row_blocks, col_blocks = D // TB, FF // TB
+    grad_scale = 1.0 / math.sqrt(tokens.shape[0] * lax.axis_size("fsdp") * lax.axis_size("rep"))
     places = jnp.stack([tile_rows, tile_cols], 1).astype(BF)
     pay = jnp.concatenate(
         [
@@ -440,43 +636,10 @@
     )
     full, tok_s, grad_s = gather(pay, tokens, grad_out)
     full = full.reshape(2, 64, GROWS, TB)
-    left_all = full[:, :, :LEFT].reshape(2, D, TB).transpose(1, 0, 2).reshape(D, R)
-    right_all = full[:, :, LEFT : LEFT + RIGHT].reshape(2, FF, TB).transpose(1, 0, 2).reshape(FF, R)
-    tiles_all = full[:, :, LEFT + RIGHT : QROWS].transpose(1, 0, 2, 3).reshape(128, TB, TB)
-    index = full[:, :, QROWS, :2].astype(jnp.int32)
-    rows_all = index[:, :, 0].T.reshape(128)
-    cols_all = index[:, :, 1].T.reshape(128)
-
-    both_tok = jnp.concatenate([tokens, tok_s], 0)
-    both_grad = jnp.concatenate([grad_out, grad_s], 0)
-    latent2 = jnp.dot(both_tok, left_all, preferred_element_type=F32).astype(BF)
-    back2 = jnp.dot(both_grad, right_all, preferred_element_type=F32).astype(BF)
-    latent, latent_grad = latent2[:here], back2[:here]
-
-    token_tiles = jnp.take(tokens.reshape(here, row_blocks, TB), rows_all, axis=1)
-    tile_prod = jnp.einsum("tkc,kcd->tkd", token_tiles, tiles_all, preferred_element_type=F32)
-    sparse_out = jnp.zeros((here, col_blocks, TB), F32).at[:, cols_all].add(tile_prod).reshape(here, FF)
-    out_rows = (contract_cols(latent, right_all) + sparse_out).astype(BF)
-    grad_tiles = jnp.take(grad_out.reshape(here, col_blocks, TB), cols_all, axis=1)
-    tile_back = jnp.einsum("tkd,kcd->tkc", grad_tiles, tiles_all, preferred_element_type=F32)
-    sparse_back = jnp.zeros((here, row_blocks, TB), F32).at[:, rows_all].add(tile_back).reshape(here, D)
-    input_grad = (contract_cols(latent_grad, left_all) + sparse_back).astype(BF)
-
-    lat_h = lax.dynamic_slice_in_dim(latent2, core * TB, TB, 1)
-    back_h = lax.dynamic_slice_in_dim(back2, core * TB, TB, 1)
-    rows_h = lax.dynamic_index_in_dim(index[:, :, 0], core, 0, False)
-    cols_h = lax.dynamic_index_in_dim(index[:, :, 1], core, 0, False)
-    tok_h = jnp.take(both_tok.reshape(2 * here, row_blocks, TB), rows_h, axis=1)
-    grad_h = jnp.take(both_grad.reshape(2 * here, col_blocks, TB), cols_h, axis=1)
-    q = jnp.concatenate(
-        [
-            contract_rows(both_tok, back_h).astype(BF).reshape(64, LEFT, TB),
-            contract_rows(both_grad, lat_h).astype(BF).reshape(64, RIGHT, TB),
-            jnp.einsum("tkc,tkd->kcd", tok_h, grad_h, preferred_element_type=F32).astype(BF),
-        ],
-        1,
-    ).reshape(SIDE, SIDE, SIDE, QROWS, TB)
-    total = reduce(q, grad_scale)
+    places_all = full[:, :, QROWS, :2].astype(jnp.int32).transpose(2, 1, 0).reshape(2, 128)
+    total, out_rows, input_grad = products(
+        places_all, *sorted_tiles(places_all), full, tokens, tok_s, grad_out, grad_s, grad_scale
+    )
     left_grad = total[:, :LEFT].transpose(1, 0, 2).reshape(LEFT, R)
     right_grad = total[:, LEFT : LEFT + RIGHT].transpose(0, 2, 1).reshape(R, RIGHT)
     return (out_rows, input_grad, left_grad, right_grad, total[:, LEFT + RIGHT :])

time: 312 us -> 162 us (0.52)
  local copies, waits for them, and re-layouts: 84.6 us -> 13.4 us
  matrix products: 48.8 us -> 0 us
  other arithmetic: 47.4 us -> 5.63 us
  Pallas kernels: 129 us -> 142 us
    dot_general x9 -> x0, matrix products: 48.8 us -> none  [the longest x2 11.3 us: contract_cols(): lax.dot_general(left, right, (((1,), (1,)), ((), ())), preferred_element_...]
    scatter-add x2 -> x0, other arithmetic: 43.3 us -> none  [the longest x1 26.3 us: local(): jnp.zeros((here, col_blocks, TB), F32).at[:, cols_all].add(tile_prod)]
    pallas_call x1, Pallas kernels: 58.4 us -> 83.3 us  [products(): pl.pallas_call(lambda *refs: products_kernel(scale, *refs), out_shape=(ja...]
    gather x4 -> x0, local copies, waits for them, and re-layouts: 19.1 us -> none  [the longest x1 6.23 us: local(): jnp.take(both_grad.reshape(2 * here, col_blocks, TB), cols_h, axis=1)]
    transpose x6 -> x1, local copies, waits for them, and re-layouts: 17.3 us -> 0.52 us  [local(): full[:, :, QROWS, :2].astype(jnp.int32).transpose(2, 1, 0).reshape(2, 128)]
    reshape x8 -> x1, local copies, waits for them, and re-layouts: 14 us -> 0.71 us  [local(): full[:, :, QROWS, :2].astype(jnp.int32).transpose(2, 1, 0).reshape(2, 128)]
    pallas_call x1, Pallas kernels: 70.2 us -> 58.3 us  [gather(): pl.pallas_call(gather_kernel, out_shape=(jax.ShapeDtypeStruct((2, SIDE, S...]
    unnamed x23 -> x7, local copies, waits for them, and re-layouts: 15.7 us -> 5.38 us
where the time goes in v2:
time: 162 us; the launch traced here: 161 us
  Pallas kernels  142 us (88%)
  local copies, waits for them, and re-layouts  13.4 us (8%)
  other arithmetic  5.63 us (3%)
    pallas_call x1, Pallas kernels, products(): pl.pallas_call(lambda *refs: products_kernel(scale, *refs), out_shape=(ja...  83.3 us
    pallas_call x1, Pallas kernels, gather(): pl.pallas_call(gather_kernel, out_shape=(jax.ShapeDtypeStruct((2, SIDE, S...  58.3 us
    unnamed x7, local copies, waits for them, and re-layouts  5.38 us

profile of v2, /device:TPU:1, one launch (start us, length us, event | category | flops | bytes accessed | tf_op | source)
XLA Modules:
  0.0 161.4 jit_solution(6179227335209307190)
XLA Ops:
  0.6 0.0 copy-start
  0.6 0.7 convert_bitcast_fusion
  1.4 0.1 copy.31
  1.5 0.8 bitcast_bitcast_fusion.1
  2.3 0.0 copy-done
  2.3 1.5 pad_maximum_fusion.pay
  3.8 58.3 %gather_factors.1 = (bf16[2,4,4,4,432,128]{5,4,3,2,1,0:T(8,128)(2,1)}, bf16[128,4096]{1,0:T(8,128)(2,1)}, bf16[128,14336]{1,0:T(8,128)(2,1)}) custom-call(bf16[2,432,128]{2,1,0:T(8,128)(2,1)} %pad_maximum_fusion.pay, bf16[128,4096]{1,0:T(8,128)(2,1)} %refs_4_.1, bf16[128,14336]{1,0:T(8,128)(2,1)} %refs_6_.1), custom_call_target="tpu_custom_call" | custom-call | tf_op jit(solution)/shard_map/gather_factors/pallas_call | solution.py:250
  62.1 1.0 slice_convert_fusion
  63.1 0.5 copy.26
  63.7 0.7 reshape.136.refs_0_
  64.4 0.1 fusion.4
  64.4 0.5 copy.27
  64.9 0.1 squeeze.2
  65.1 0.1 fusion
  65.2 0.2 convert_reduce_fusion.3
  65.4 0.5 copy.28
  65.9 0.1 broadcast_in_dim.76
  66.0 0.2 convert_reduce_fusion.1
  66.2 0.1 fusion.1
  66.3 0.3 select_reduce_fusion.1
  66.6 0.1 slice_compare_fusion.1
  66.7 0.1 fusion.2
  66.8 0.1 slice_compare_fusion
  66.9 0.1 fusion.3
  66.9 0.6 add_convert_fusion.refs_2_
  67.5 0.6 pad_add_fusion.refs_1_
  68.1 83.3 %products_and_reduction.1 = (f32[2,416,128]{2,1,0:T(8,128)}, bf16[128,14336]{1,0:T(8,128)(2,1)}, bf16[128,4096]{1,0:T(8,128)(2,1)}) custom-call(s32[2,128]{1,0:T(2,128)} %reshape.136.refs_0_, s32[2,4,128]{2,1,0:T(4,128)} %pad_add_fusion.refs_1_, f32[2,128]{1,0:T(2,128)} %add_convert_fusion.refs_2_, bf16[2,64,432,128]{3,2,1,0:T(8,128)(2,1)} %bitcast.54, ...), custom_call_target="tpu_custom_call" | custom-call | tf_op jit(solution)/shard_map/products_and_reduction/pallas_call | solution.py:572
  151.4 1.5 copy_bitcast_fusion.1
  152.9 1.6 slice.43
  154.5 1.6 %copy_bitcast_fusion = f32[256,224]{0,1:T(8,128)} fusion(f32[2,416,128]{2,1,0:T(8,128)} %get-tuple-element.16), kind=kLoop, calls=%fused_computation | loop fusion | bytes 458752 | tf_op jit(solution)/shard_map/reshape | solution.py:644
  156.1 4.3 %copy.42 = bf16[128,14336]{1,0:T(8,128)(2,1)} copy(bf16[128,14336]{1,0:T(8,128)(2,1)} %get-tuple-element.38) | data formatting | bytes 7340032
  160.4 1.0 copy.43
  (13 shorter events, 0.1 us)
Async XLA Ops:
  0.6 1.6 %copy-start = (bf16[256,224]{0,1:T(8,128)(2,1)S(1)}, bf16[256,224]{0,1:T(8,128)(2,1)}, u32[]{:S(2)}) copy-start(bf16[256,224]{0,1:T(8,128)(2,1)} %param.9) | copy-start | bytes 344068
  156.1 4.3 %copy-start.1 = (bf16[128,4096]{1,0:T(8,128)(2,1)S(1)}, bf16[128,4096]{1,0:T(8,128)(2,1)}, u32[]{:S(2)}) copy-start(bf16[128,4096]{1,0:T(8,128)(2,1)} %get-tuple-element.39) | copy-start | bytes 3145732

commit v3 on v2

--- a/solution.py
+++ b/solution.py
@@ -14,7 +14,6 @@
 SIDE = 4
 LEFT = 64
 RIGHT = 224
-GROWS = LEFT + RIGHT + TB + 16
 QROWS = LEFT + RIGHT + TB
 MESH = pl.DeviceIdType.MESH
 BF = jnp.bfloat16
@@ -99,16 +98,7 @@
     return ref.at[sel[0], sel[1], sel[2], pl.ds(r0, n), :]
 
 
-GATHER = (((X, Y, H), 0, 80), ((Y, H, X), 80, 176), ((H, X, Y), 256, 176))
-
-
-def run_all(active):
-    while active:
-        for run in list(active):
-            try:
-                next(run)
-            except StopIteration:
-                active.remove(run)
+GATHER = (((X, Y, H), 0, 128), ((Y, H, X), 128, 144), ((H, X, Y), 272, 144))
 
 
 def spread(me, axis, send, got, ready):
@@ -170,105 +160,7 @@
         ready(across)
 
 
-def gather_kernel(pay, tok, grad, full, tok_s, grad_s, send_sems, recv_sems, local_sem, side_sems, wide_sems):
-    me = Place()
-    mine = full.at[me.c]
-    own = pltpu.make_async_copy(pay.at[me.c], mine.at[me.at[0], me.at[1], me.at[2]], local_sem)
-    own.start()
-    me.greet()
-    own.wait()
-    wire = Wire(send_sems, recv_sems)
-    active = []
-
-    def to_sibling(src, dst, pair):
-        return pltpu.make_async_remote_copy(
-            src_ref=src,
-            dst_ref=dst,
-            send_sem=pair.at[0],
-            recv_sem=pair.at[1],
-            device_id=me.sib,
-            device_id_type=MESH,
-        )
-
-    def part(order, row0, rows):
-        one, two, three = order
-
-        def piece(at, half=None):
-            sel = [at.get(a, slice(None)) for a in range(3)]
-            if half is not None:
-                sel[one] = pl.ds(half * 2, 2)
-            return mine.at[sel[0], sel[1], sel[2], pl.ds(row0, rows), :]
-
-        def last(j2):
-            def send(j, half, device):
-                ref = piece({two: j2, three: j}, half)
-                return wire(ref, ref, device)
-
-            def got(j, half):
-                ref = piece({two: j2, three: j}, half)
-                to_sibling(ref, ref, side_sems).start()
-
-            ref = piece({two: j2, three: me.at[three]})
-            to_sibling(ref, ref, side_sems).start()
-            return spread(me, three, send, got, lambda j: None)
-
-        def start_last(j2):
-            run = last(j2)
-            next(run)
-            active.append(run)
-
-        def send(j, half, device):
-            ref = piece({two: j, three: me.at[three]}, half)
-            return wire(ref, ref, device)
-
-        seed = piece({a: me.at[a] for a in range(3)})
-        seeds = [wire(seed, seed, device) for device in me.direct[one]]
-        yield
-        for copy in seeds:
-            copy.wait_recv()
-        run = spread(me, two, send, lambda j, half: None, start_last)
-        next(run)
-        start_last(me.at[two])
-        active.append(run)
-
-    for p in GATHER:
-        active.append(part(*p))
-    for run in active:
-        next(run)
-    swaps = [to_sibling(tok, tok_s, wide_sems.at[0]), to_sibling(grad, grad_s, wide_sems.at[1])]
-    for swap in swaps:
-        swap.start()
-    run_all(active)
-    wire.finish()
-    for swap in swaps:
-        swap.wait()
-    whole = to_sibling(mine, full.at[1 - me.c], side_sems)
-    whole.wait()
-
-
-def gather(pay, tok, grad):
-    return pl.pallas_call(
-        gather_kernel,
-        out_shape=(
-            jax.ShapeDtypeStruct((2, SIDE, SIDE, SIDE, GROWS, TB), BF),
-            jax.ShapeDtypeStruct(tok.shape, BF),
-            jax.ShapeDtypeStruct(grad.shape, BF),
-        ),
-        in_specs=[ANY] * 3,
-        out_specs=(ANY,) * 3,
-        scratch_shapes=[
-            pltpu.SemaphoreType.DMA((120,)),
-            pltpu.SemaphoreType.DMA((120,)),
-            pltpu.SemaphoreType.DMA,
-            pltpu.SemaphoreType.DMA((2,)),
-            pltpu.SemaphoreType.DMA((2, 2)),
-        ],
-        compiler_params=pltpu.CompilerParams(collective_id=0, has_side_effects=True),
-        name="gather_factors",
-    )(pay, tok, grad)
-
-
-REDUCE = (((H, Y, X), 0, 144), ((X, H, Y), 144, 144), ((Y, X, H), 288, 128))
+REDUCE = (((H, Y, X), 0, 96), ((X, H, Y), 96, 96), ((Y, X, H), 192, 96), ((Y, X, H), 288, 128))
 
 
 def add_into(dst, *terms):
@@ -300,7 +192,7 @@
 def reduce_parts(me, scale, q_ref, out, scratch):
     (send_sems, recv_sems), scratch = scratch[:2], scratch[2:]
     wire = Wire(send_sems, recv_sems)
-    per_part = len(scratch) // 3
+    per_part = len(scratch) // len(REDUCE)
 
     def part(n):
         order, row0, rows = REDUCE[n]
@@ -394,7 +286,19 @@
         yield
         final.wait_recv()
 
-    return [part(n) for n in range(3)] + [wire.finish]
+    return [part(n) for n in range(len(REDUCE))] + [wire.finish]
+
+
+def run_with(active, work):
+    while active:
+        for run in list(active):
+            try:
+                next(run)
+            except StopIteration:
+                active.remove(run)
+        next(work, None)
+    for _ in work:
+        pass
 
 
 def reduce_scratch():
@@ -413,18 +317,6 @@
     return shapes
 
 
-def run_with(active, work):
-    while active:
-        for run in list(active):
-            try:
-                next(run)
-            except StopIteration:
-                active.remove(run)
-        next(work, None)
-    for _ in work:
-        pass
-
-
 CHUNKS = 8
 PER = 64 // CHUNKS
 WIDE = PER * RIGHT
@@ -455,84 +347,238 @@
     return copy
 
 
-def products_kernel(scale, places, order, same, full, tok, tok_s, grad, grad_s, total, out, back_out, *scratch):
-    (q, left, right, tiles, tok2, grad2, run, latent, latent_o, back_c, back_o, stage) = scratch[:12]
-    left_sems, right_sems, tile_sem, stage_sems = scratch[12:16]
+def within(index, count):
+    return jnp.minimum(jnp.maximum(index, 0), count - 1)
+
+
+def sort_tiles(marks, order, joins):
+    held = marks[...].reshape(64 * 16, TB)
+    i0 = lax.broadcasted_iota(jnp.int32, (128, 1024), 0)
+    i1 = lax.broadcasted_iota(jnp.int32, (128, 1024), 1)
+    columns, rows = [], []
+    for base in (0, 8):
+        pick = (i1 == (i0 >> 1) * 16 + (i0 & 1) * 4 + base).astype(F32).astype(BF)
+        columns.append(dot(pick, held))
+        rows.append(lax.dot_general(held, pick, (((0,), (1,)), ((), ())), preferred_element_type=F32))
+    t0 = lax.broadcasted_iota(jnp.int32, (128, 128), 0).astype(F32)
+    t1 = lax.broadcasted_iota(jnp.int32, (128, 128), 1).astype(F32)
+    s8 = lax.broadcasted_iota(jnp.int32, (8, 128), 0)
+    lane = lax.broadcasted_iota(jnp.int32, (8, 128), 1)
+    one = lambda truth: jnp.where(truth, 1.0, 0.0)
+    for which, key in ((0, 1), (1, 0)):
+        by0, by1, other = columns[key], rows[key], rows[1 - key]
+        rank = jnp.sum(one(by1 * 128 + t1 < by0 * 128 + t0), 1, keepdims=True)
+        moved = one(rank == t1).astype(BF)
+        earlier = jnp.max(one(by0 == by1) * one(t0 < t1), 0, keepdims=True)
+        upto = jnp.sum(one(by0 <= t1), 0, keepdims=True)
+        present = jnp.max(one(by0 == t1), 0, keepdims=True)
+        slot = jnp.where(present > 0.5, upto - 1, float(EMPTY))
+        value = jnp.where(s8 == 0, other[:8], 0.0)
+        value = jnp.where(s8 == 1, (lane & 1).astype(F32), value)
+        value = jnp.where(s8 == 2, (lane >> 1).astype(F32), value)
+        value = jnp.where(s8 == 4, jnp.broadcast_to(earlier, (8, 128)), value)
+        found = dot(value.astype(BF), moved)
+        found = jnp.where(s8 == 3, jnp.broadcast_to(slot, (8, 128)), found)
+        order[which] = found.astype(jnp.int32)
+        joins[which] = found
+    order[2] = jnp.where(s8 == 0, rows[0][:8], rows[1][:8]).astype(jnp.int32)
+
+
+def kernel(scale, pay, mark, tok, grad, total, out, back_out, full, tok_s, grad_s, *scratch):
+    (q, left, right, tiles, tok2, grad2, run, latent, latent_o, back_c, back_o, stage, out_v, back_v) = scratch[:14]
+    (marks, order_v, joins_v, order, joins) = scratch[14:19]
+    left_sems, right_sems, tile_sem, stage_sems, order_sems, out_sem, back_sem = scratch[19:26]
+    send_sems, recv_sems, local_sems, side_sems, wide_sems = scratch[26:31]
     me = Place()
     c, o = me.c, 1 - me.c
     here = tok.shape[0]
+    mine = full.at[c]
+    at = me.at
+    own = [
+        load(pay.at[c], mine.at[at[0], at[1], at[2]], local_sems.at[0]),
+        load(mark, marks.at[at[0], at[1], at[2]], local_sems.at[1]),
+    ]
+    me.greet()
+    for copy in own:
+        copy.wait()
+    wire = Wire(send_sems, recv_sems)
+    active = []
+    known = set()
+
+    def to_sibling(src, dst, pair):
+        return pltpu.make_async_remote_copy(
+            src_ref=src,
+            dst_ref=dst,
+            send_sem=pair.at[0],
+            recv_sem=pair.at[1],
+            device_id=me.sib,
+            device_id_type=MESH,
+        )
+
+    def positions():
+        for seg, axis in (
+            (marks.at[at[0], at[1], at[2]], H),
+            (marks.at[at[0], :, at[2]], X),
+            (marks.at[at[0]], Y),
+        ):
+            copies = [wire(seg, seg, device) for device in me.direct[axis]]
+            yield
+            for copy in copies:
+                copy.wait_recv()
+        known.add("marks")
+
+    def part(order3, row0, rows):
+        one, two, three = order3
+
+        def piece(sel, half=None):
+            sel = [sel.get(a, slice(None)) for a in range(3)]
+            if half is not None:
+                sel[one] = pl.ds(half * 2, 2)
+            return mine.at[sel[0], sel[1], sel[2], pl.ds(row0, rows), :]
+
+        def last(j2):
+            def send(j, half, device):
+                ref = piece({two: j2, three: j}, half)
+                return wire(ref, ref, device)
+
+            def got(j, half):
+                ref = piece({two: j2, three: j}, half)
+                to_sibling(ref, ref, side_sems).start()
+
+            ref = piece({two: j2, three: at[three]})
+            to_sibling(ref, ref, side_sems).start()
+            return spread(me, three, send, got, lambda j: None)
+
+        def start_last(j2):
+            nonlocal_run = last(j2)
+            next(nonlocal_run)
+            active.append(nonlocal_run)
+
+        def send(j, half, device):
+            ref = piece({two: j, three: at[three]}, half)
+            return wire(ref, ref, device)
+
+        seed = piece({a: at[a] for a in range(3)})
+        seeds = [wire(seed, seed, device) for device in me.direct[one]]
+        yield
+        for copy in seeds:
+            copy.wait_recv()
+        spreading = spread(me, two, send, lambda j, half: None, start_last)
+        next(spreading)
+        start_last(at[two])
+        active.append(spreading)
+
+    active.append(positions())
+    for p in GATHER:
+        active.append(part(*p))
+    for each in active:
+        next(each)
+    swaps = [to_sibling(tok, tok_s, wide_sems.at[0]), to_sibling(grad, grad_s, wide_sems.at[1])]
+    for swap in swaps:
+        swap.start()
+    sums = reduce_parts(me, scale, q, total, scratch[31:])
     pieces = [(tok, tok_s, tok2, n) for n in range(D // PIECE)] + [(grad, grad_s, grad2, n) for n in range(FF // PIECE)]
 
     def fetch(k):
-        own, other, _, n = pieces[k]
+        first, second, _, n = pieces[k]
         span = pl.ds(n * PIECE, PIECE)
         return [
-            load(own.at[:, span], stage.at[k % 3, pl.ds(0, here)], stage_sems.at[0, k % 3]),
-            load(other.at[:, span], stage.at[k % 3, pl.ds(here, here)], stage_sems.at[1, k % 3]),
+            load(first.at[:, span], stage.at[k % 3, pl.ds(0, here)], stage_sems.at[0, k % 3]),
+            load(second.at[:, span], stage.at[k % 3, pl.ds(here, here)], stage_sems.at[1, k % 3]),
         ]
-
-    coming = [fetch(k) for k in range(3)]
-    left_in, right_in = [], []
-    for k, half in enumerate((c, o)):
-        left_in.append(load(full.at[half, :, pl.ds(0, LEFT), :], left.at[k], left_sems.at[k]))
-        right_in.append(load(full.at[half, :, pl.ds(LEFT, RIGHT), :], right.at[k], right_sems.at[k]))
-    tiles_in = load(full.at[:, :, pl.ds(LEFT + RIGHT, TB), :], tiles, tile_sem)
-    me.greet()
-    runs = reduce_parts(me, scale, q, total, scratch[16:])
 
     def tile_part(g, _):
         for u in range(8):
             t = 2 * (g * 8 + u) + c
-            part = contract_rows(tok2[places[0, t]], grad2[places[1, t]])
-            q[g // 2, (g % 2) * 2 + u // 4, u % 4, LEFT + RIGHT :, :] = part.astype(BF)
+            product = contract_rows(tok2[within(order[2, 0, t], D // TB)], grad2[within(order[2, 1, t], FF // TB)])
+            q[g // 2, (g % 2) * 2 + u // 4, u % 4, LEFT + RIGHT :, :] = product.astype(BF)
         return 0
 
-    for k, (_, _, held, n) in enumerate(pieces):
-        for copy in coming[k]:
+    def early():
+        yield
+        yield
+        for swap in swaps:
+            swap.wait_recv()
+        coming = [fetch(k) for k in range(3)]
+        for k, (_, _, held, n) in enumerate(pieces):
+            for copy in coming[k]:
+                copy.wait()
+            for b in range(PIECE // TB):
+                held[n * (PIECE // TB) + b] = stage[k % 3, :, b * TB : (b + 1) * TB]
+            if k + 3 < len(pieces):
+                coming.append(fetch(k + 3))
+            if k % 3 == 2:
+                yield
+        while "marks" not in known:
+            yield
+        sort_tiles(marks, order_v, joins_v)
+        filed = [load(order_v, order, order_sems.at[0]), load(joins_v, joins, order_sems.at[1])]
+        for copy in filed:
             copy.wait()
-        for b in range(PIECE // TB):
-            held[n * (PIECE // TB) + b] = stage[k % 3, :, b * TB : (b + 1) * TB]
-        if k + 3 < len(pieces):
-            coming.append(fetch(k + 3))
-    lax.fori_loop(0, 8, tile_part, 0)
-    next(runs[2])
-
+        yield
+        for n in range(2):
+            lax.fori_loop(n * 4, n * 4 + 4, tile_part, 0)
+            yield
+        next(sums[3])
+        summing.append(sums[3])
+
+    summing = []
+    before = early()
+    while active:
+        for each in list(active) + list(summing):
+            if next(each, "end") == "end":
+                (active if each in active else summing).remove(each)
+        next(before, None)
+    for _ in before:
+        pass
+    left_in = [load(full.at[c, :, :, :, pl.ds(0, LEFT), :], left.at[0], left_sems.at[0])]
+    right_in = [load(full.at[c, :, :, :, pl.ds(LEFT, RIGHT), :], right.at[0], right_sems.at[0])]
     left_in[0].wait()
     latent[...] = dot(wide(tok2, 0, D // TB), left[0].reshape(D, TB)).astype(BF)
     right_in[0].wait()
     back = jnp.zeros((2 * here, TB), F32)
     for j in range(CHUNKS):
-        part = wide(grad2, j * WIDE // TB, WIDE // TB)
-        back = back + dot(part, right[0, j * PER : (j + 1) * PER].reshape(WIDE, TB))
-        q[j // 2, (j % 2) * 2 : (j % 2) * 2 + 2, :, LEFT : LEFT + RIGHT, :] = (
-            contract_rows(part, latent[...]).astype(BF).reshape(2, 4, RIGHT, TB)
-        )
-    next(runs[1])
+        cots = wide(grad2, j * WIDE // TB, WIDE // TB)
+        y, h = j // 2, slice((j % 2) * 2, (j % 2) * 2 + 2)
+        back = back + dot(cots, right[0, y, h].reshape(WIDE, TB))
+        q[y, h, :, LEFT : LEFT + RIGHT, :] = contract_rows(cots, latent[...]).astype(BF).reshape(2, 4, RIGHT, TB)
+    next(sums[1])
+    next(sums[2])
     back_c[...] = back.astype(BF)
     for j in range(4):
-        part = contract_rows(wide(tok2, j * 8, 8), back_c[...])
-        q[j, :, :, :LEFT, :] = part.astype(BF).reshape(4, 4, LEFT, TB)
-    next(runs[0])
+        product = contract_rows(wide(tok2, j * 8, 8), back_c[...])
+        q[j, :, :, :LEFT, :] = product.astype(BF).reshape(4, 4, LEFT, TB)
+    next(sums[0])
+    to_sibling(mine, full.at[o], side_sems).wait()
+    left_in.append(load(full.at[o, :, :, :, pl.ds(0, LEFT), :], left.at[1], left_sems.at[1]))
+    right_in.append(load(full.at[o, :, :, :, pl.ds(LEFT, RIGHT), :], right.at[1], right_sems.at[1]))
+    for n in range(16):
+        load(full.at[:, n // 4, n % 4, :, pl.ds(LEFT + RIGHT, TB), :], tiles.at[:, pl.ds(4 * n, 4)], tile_sem)
+    tiles_in = pltpu.make_async_copy(tiles, tiles, tile_sem)
 
     def running_sums(which, product, g0):
         def body(g, held):
             parts = [product(g * 8 + u) for u in range(8)]
             for u in range(8):
                 t = g * 8 + u
-                held = held * same[which, t] + parts[u]
+                held = held * joins[which, 4, t] + parts[u]
                 run[t] = held
             return held
 
-        before = jnp.zeros((here, TB), F32) if g0 == 0 else run[g0 * 8 - 1]
-        lax.fori_loop(g0, g0 + 16 // SLICES, body, before)
+        first = jnp.zeros((here, TB), F32) if g0 == 0 else run[g0 * 8 - 1]
+        lax.fori_loop(g0, g0 + 16 // SLICES, body, first)
+
+    def tile(which, t):
+        return tiles[within(order[which, 1, t], 2), within(order[which, 2, t], 64)]
 
     def ahead(t):
-        return dot(tok2[order[0, 0, t], :here], tiles[order[0, 1, t], order[0, 2, t]])
+        return dot(tok2[within(order[0, 0, t], D // TB), :here], tile(0, t))
 
     def behind(t):
-        return contract_cols(grad2[order[1, 0, t], :here], tiles[order[1, 1, t], order[1, 2, t]])
+        return contract_cols(grad2[within(order[1, 0, t], FF // TB), :here], tile(1, t))
 
     def work():
+        yield
         left_in[1].wait()
         latent_o[...] = dot(wide(tok2, 0, D // TB, here), left[1].reshape(D, TB)).astype(BF)
         tiles_in.wait()
@@ -543,45 +589,57 @@
         right_in[1].wait()
         back_o[...] = jnp.zeros((here, TB), F32)
         for j in range(CHUNKS):
-            rights = [right[k, j * PER : (j + 1) * PER].reshape(WIDE, TB) for k in (0, 1)]
+            span = slice(j * WIDE, (j + 1) * WIDE)
+            y, h = j // 2, slice((j % 2) * 2, (j % 2) * 2 + 2)
+            rights = [right[k, y, h].reshape(WIDE, TB) for k in (0, 1)]
             back_o[...] += dot(wide(grad2, j * WIDE // TB, WIDE // TB, here), rights[1])
             dense = contract_cols(latent[:here], rights[0]) + contract_cols(latent_o[...], rights[1])
             for b in range(WIDE // TB):
                 n = j * (WIDE // TB) + b
-                out[:, n * TB : (n + 1) * TB] = (dense[:, b * TB : (b + 1) * TB] + run[order[0, 3, n]]).astype(BF)
+                out_v[:, n * TB : (n + 1) * TB] = (dense[:, b * TB : (b + 1) * TB] + run[within(order[0, 3, n], EMPTY + 1)]).astype(BF)
+            pltpu.make_async_copy(out_v.at[:, span], out.at[:, span], out_sem).start()
             yield
         for n in range(SLICES):
             running_sums(1, behind, n * 16 // SLICES)
             yield
         back_h = back_o[...].astype(BF)
         for j in range(4):
-            lefts = [left[k, j * 16 : (j + 1) * 16].reshape(1024, TB) for k in (0, 1)]
+            lefts = [left[k, j].reshape(1024, TB) for k in (0, 1)]
             dense = contract_cols(back_c[:here], lefts[0]) + contract_cols(back_h, lefts[1])
             for b in range(8):
                 n = j * 8 + b
-                back_out[:, n * TB : (n + 1) * TB] = (dense[:, b * TB : (b + 1) * TB] + run[order[1, 3, n]]).astype(BF)
+                back_v[:, n * TB : (n + 1) * TB] = (dense[:, b * TB : (b + 1) * TB] + run[within(order[1, 3, n], EMPTY + 1)]).astype(BF)
             if j % 2:
                 yield
-
-    run_with(list(runs[:3]), work())
-    runs[3]()
-
-
-def products(places, order, same, full, tok, tok_s, grad, grad_s, scale):
+        pltpu.make_async_copy(back_v, back_out, back_sem).start()
+
+    run_with(summing + [sums[0], sums[1], sums[2]], work())
+    pltpu.make_async_copy(out_v, out, out_sem).wait()
+    pltpu.make_async_copy(back_v, back_out, back_sem).wait()
+    wire.finish()
+    for swap in swaps:
+        swap.wait_send()
+    sums[4]()
+
+
+def whole_step(pay, mark, tok, grad, scale):
     here = tok.shape[0]
     return pl.pallas_call(
-        lambda *refs: products_kernel(scale, *refs),
+        lambda *refs: kernel(scale, *refs),
         out_shape=(
             jax.ShapeDtypeStruct((2, QROWS, TB), F32),
             jax.ShapeDtypeStruct((here, FF), BF),
             jax.ShapeDtypeStruct((here, D), BF),
+            jax.ShapeDtypeStruct((2, SIDE, SIDE, SIDE, QROWS, TB), BF),
+            jax.ShapeDtypeStruct(tok.shape, BF),
+            jax.ShapeDtypeStruct(grad.shape, BF),
         ),
-        in_specs=[pl.BlockSpec(memory_space=pltpu.SMEM)] * 3 + [ANY] * 5,
-        out_specs=(VMEM,) * 3,
+        in_specs=[ANY] * 4,
+        out_specs=(VMEM,) + (ANY,) * 5,
         scratch_shapes=[
             pltpu.VMEM((SIDE, SIDE, SIDE, QROWS, TB), BF),
-            pltpu.VMEM((2, 64, LEFT, TB), BF),
-            pltpu.VMEM((2, 64, RIGHT, TB), BF),
+            pltpu.VMEM((2, SIDE, SIDE, SIDE, LEFT, TB), BF),
+            pltpu.VMEM((2, SIDE, SIDE, SIDE, RIGHT, TB), BF),
             pltpu.VMEM((2, 64, TB, TB), BF),
             pltpu.VMEM((D // TB, 2 * here, TB), BF),
             pltpu.VMEM((FF // TB, 2 * here, TB), BF),
@@ -591,55 +649,49 @@
             pltpu.VMEM((2 * here, TB), BF),
             pltpu.VMEM((here, TB), F32),
             pltpu.VMEM((3, 2 * here, PIECE), BF),
+            pltpu.VMEM((here, FF), BF),
+            pltpu.VMEM((here, D), BF),
+            pltpu.VMEM((SIDE, SIDE, SIDE, 16, TB), BF),
+            pltpu.VMEM((3, 8, TB), jnp.int32),
+            pltpu.VMEM((2, 8, TB), F32),
+            pltpu.SMEM((3, 8, TB), jnp.int32),
+            pltpu.SMEM((2, 8, TB), F32),
             pltpu.SemaphoreType.DMA((2,)),
             pltpu.SemaphoreType.DMA((2,)),
             pltpu.SemaphoreType.DMA,
             pltpu.SemaphoreType.DMA((2, 3)),
-            pltpu.SemaphoreType.DMA((80,)),
-            pltpu.SemaphoreType.DMA((80,)),
+            pltpu.SemaphoreType.DMA((2,)),
+            pltpu.SemaphoreType.DMA,
+            pltpu.SemaphoreType.DMA,
+            pltpu.SemaphoreType.DMA((120,)),
+            pltpu.SemaphoreType.DMA((120,)),
+            pltpu.SemaphoreType.DMA((2,)),
+            pltpu.SemaphoreType.DMA((2,)),
+            pltpu.SemaphoreType.DMA((2, 2)),
+            pltpu.SemaphoreType.DMA((100,)),
+            pltpu.SemaphoreType.DMA((100,)),
         ]
         + reduce_scratch(),
         compiler_params=pltpu.CompilerParams(
-            collective_id=1, has_side_effects=True, vmem_limit_bytes=62 * 1024 * 1024
+            collective_id=0, has_side_effects=True, vmem_limit_bytes=63 * 1024 * 1024
         ),
-        name="products_and_reduction",
-    )(places, order, same, full, tok, tok_s, grad, grad_s)
-
-
-def sorted_tiles(places):
-    ids = jnp.arange(128, dtype=jnp.int32)
-    found, joins = [], []
-    for key, other in ((places[1], places[0]), (places[0], places[1])):
-        unique = key * 128 + ids
-        rank = jnp.sum((unique[None, :] < unique[:, None]).astype(jnp.int32), 1)
-        at = rank[None, :] == ids[:, None]
-        pick = lambda v: jnp.sum(jnp.where(at, v[None, :], 0), 1)
-        by = pick(key)
-        joins.append(jnp.concatenate([jnp.zeros((1,), F32), (by[1:] == by[:-1]).astype(F32)]))
-        upto = jnp.sum((key[None, :] <= ids[:, None]).astype(jnp.int32), 1)
-        present = jnp.any(key[None, :] == ids[:, None], 1)
-        found.append(jnp.stack([pick(other), pick(ids % 2), pick(ids // 2), jnp.where(present, upto - 1, EMPTY)]))
-    return jnp.stack(found), jnp.stack(joins)
+        name="whole_step",
+    )(pay, mark, tok, grad)
 
 
 def local(tokens, left_factor, right_factor, tile_values, tile_rows, tile_cols, grad_out):
     grad_scale = 1.0 / math.sqrt(tokens.shape[0] * lax.axis_size("fsdp") * lax.axis_size("rep"))
-    places = jnp.stack([tile_rows, tile_cols], 1).astype(BF)
+    mark = jnp.repeat(jnp.concatenate([tile_rows, tile_cols]).astype(BF), 4)
+    mark = jnp.broadcast_to(mark[:, None], (16, TB))
     pay = jnp.concatenate(
         [
             left_factor.reshape(LEFT, 2, TB).transpose(1, 0, 2),
             right_factor.T.reshape(RIGHT, 2, TB).transpose(1, 0, 2),
             tile_values,
-            jnp.broadcast_to(jnp.pad(places, ((0, 0), (0, TB - 2)))[:, None, :], (2, 16, TB)),
         ],
         1,
     )
-    full, tok_s, grad_s = gather(pay, tokens, grad_out)
-    full = full.reshape(2, 64, GROWS, TB)
-    places_all = full[:, :, QROWS, :2].astype(jnp.int32).transpose(2, 1, 0).reshape(2, 128)
-    total, out_rows, input_grad = products(
-        places_all, *sorted_tiles(places_all), full, tokens, tok_s, grad_out, grad_s, grad_scale
-    )
+    total, out_rows, input_grad, *_ = whole_step(pay, mark, tokens, grad_out, grad_scale)
     left_grad = total[:, :LEFT].transpose(1, 0, 2).reshape(LEFT, R)
     right_grad = total[:, LEFT : LEFT + RIGHT].transpose(0, 2, 1).reshape(R, RIGHT)
     return (out_rows, input_grad, left_grad, right_grad, total[:, LEFT + RIGHT :])

time: 162 us -> 142 us (0.88)
  Pallas kernels: 142 us -> 126 us
  other arithmetic: 5.63 us -> 2.97 us
  local copies, waits for them, and re-layouts: 13.4 us -> 11.6 us
    pallas_call x2 -> x1, Pallas kernels: 142 us -> 126 us  [whole_step(): pl.pallas_call(lambda *refs: kernel(scale, *refs), out_shape=(jax.ShapeDt...]
    unnamed x7 -> x6, local copies, waits for them, and re-layouts: 5.38 us -> 5.27 us
where the time goes in v3:
time: 142 us
  Pallas kernels  126 us (89%)
  local copies, waits for them, and re-layouts  11.6 us (8%)
  other arithmetic  2.97 us (2%)
    pallas_call x1, Pallas kernels, whole_step(): pl.pallas_call(lambda *refs: kernel(scale, *refs), out_shape=(jax.ShapeDt...  126 us
    unnamed x6, local copies, waits for them, and re-layouts  5.27 us

profile of v3, /device:TPU:1, one launch (start us, length us, event | category | flops | bytes accessed | tf_op | source)
XLA Modules:
  0.0 141.6 jit_solution(430645629733553521)
XLA Ops:
  0.6 0.0 copy-start
  0.6 0.7 convert.6
  1.3 0.7 convert.7
  2.0 0.1 pad_maximum_fusion.1
  2.1 0.1 broadcast_in_dim.10
  2.2 0.1 broadcast_in_dim.11
  2.2 0.7 broadcast_in_dim.12.refs_1_
  2.9 0.8 bitcast_bitcast_fusion.1
  3.7 0.0 copy-done
  3.7 1.5 %pad_maximum_fusion.refs_0_ = bf16[2,416,128]{2,1,0:T(8,128)(2,1)} fusion(bf16[2,128,128]{2,1,0:T(8,128)(2,1)} %param.10, bf16[2,224,128]{2,1,0:T(8,128)(2,1)S(1)} %bitcast_bitcast_fusion, bf16[2,64,128]{2,1,0:T(8,128)(2,1)S(1)} %bitcast_bitcast_fusion.1), kind=kLoop, calls=%fused_computation.2 | loop fusion | flops 638976 | bytes 425984 | tf_op jit(solution)/shard_map/concatenate | solution.py:686
  5.2 126.4 %whole_step.1 = (f32[2,416,128]{2,1,0:T(8,128)}, bf16[128,14336]{1,0:T(8,128)(2,1)}, bf16[128,4096]{1,0:T(8,128)(2,1)}, bf16[2,4,4,4,416,128]{5,4,3,2,1,0:T(8,12...) custom-call(bf16[2,416,128]{2,1,0:T(8,128)(2,1)} %pad_maximum_fusion.refs_0_, ...), custom_call_target="tpu_custom_call" | custom-call | tf_op jit(solution)/shard_map/whole_step/pallas_call | solution.py:627
  131.7 1.5 %copy_bitcast_fusion.1 = f32[64,256]{1,0:T(8,128)} fusion(f32[2,416,128]{2,1,0:T(8,128)} %get-tuple-element.10), kind=kLoop, calls=%fused_computation.4 | loop fusion | bytes 131072 | tf_op jit(solution)/shard_map/reshape | solution.py:695
  133.1 1.6 %slice.11 = f32[2,128,128]{2,1,0:T(8,128)} slice(f32[2,416,128]{2,1,0:T(8,128)} %get-tuple-element.10), slice={[0:2], [288:416], [0:128]} | slice | bytes 262144 | tf_op jit(solution)/shard_map/slice | solution.py:697
  134.7 1.6 %copy_bitcast_fusion = f32[256,224]{0,1:T(8,128)} fusion(f32[2,416,128]{2,1,0:T(8,128)} %get-tuple-element.10), kind=kLoop, calls=%fused_computation | loop fusion | bytes 458752 | tf_op jit(solution)/shard_map/reshape | solution.py:696
  136.3 0.0 copy-start.1
  136.3 4.3 %copy.26 = bf16[128,14336]{1,0:T(8,128)(2,1)} copy(bf16[128,14336]{1,0:T(8,128)(2,1)} %get-tuple-element.16) | data formatting | bytes 7340032
  140.6 0.0 copy-done.1
  140.6 1.0 copy.27
  (1 shorter events, 0.0 us)
Async XLA Ops:
  0.6 3.0 %copy-start = (bf16[256,224]{0,1:T(8,128)(2,1)S(1)}, bf16[256,224]{0,1:T(8,128)(2,1)}, u32[]{:S(2)}) copy-start(bf16[256,224]{0,1:T(8,128)(2,1)} %param.9) | copy-start | bytes 344068
  136.3 4.3 %copy-start.1 = (bf16[128,4096]{1,0:T(8,128)(2,1)S(1)}, bf16[128,4096]{1,0:T(8,128)(2,1)}, u32[]{:S(2)}) copy-start(bf16[128,4096]{1,0:T(8,128)(2,1)} %get-tuple-element.17) | copy-start | bytes 3145732

commit v4 on v3

--- a/solution.py
+++ b/solution.py
@@ -384,7 +384,7 @@
     order[2] = jnp.where(s8 == 0, rows[0][:8], rows[1][:8]).astype(jnp.int32)
 
 
-def kernel(scale, pay, mark, tok, grad, total, out, back_out, full, tok_s, grad_s, *scratch):
+def kernel(scale, tile_rows, tile_cols, left_own, right_own, tiles_own, tok, grad, out, back_out, left_grad, right_grad, tile_grad, full, tok_s, grad_s, *scratch):
     (q, left, right, tiles, tok2, grad2, run, latent, latent_o, back_c, back_o, stage, out_v, back_v) = scratch[:14]
     (marks, order_v, joins_v, order, joins) = scratch[14:19]
     left_sems, right_sems, tile_sem, stage_sems, order_sems, out_sem, back_sem = scratch[19:26]
@@ -394,13 +394,21 @@
     here = tok.shape[0]
     mine = full.at[c]
     at = me.at
-    own = [
-        load(pay.at[c], mine.at[at[0], at[1], at[2]], local_sems.at[0]),
-        load(mark, marks.at[at[0], at[1], at[2]], local_sems.at[1]),
-    ]
+    pay, total = scratch[31:33]
+    pay[:LEFT] = jnp.where(c == 0, left_own[:, :TB], left_own[:, TB:])
+    turned = right_own[pl.ds(pl.multiple_of(c * TB, TB), TB), :].astype(F32)
+    turned = jnp.concatenate([turned, jnp.zeros((TB, 2 * TB - RIGHT), F32)], 1).T
+    pay[LEFT : LEFT + RIGHT] = turned[:RIGHT].astype(BF)
+    pay[LEFT + RIGHT :] = tiles_own[c]
+    found = [ref[k].astype(F32) for ref in (tile_rows, tile_cols) for k in (0, 1)]
+    group = lax.broadcasted_iota(jnp.int32, (16, TB), 0) // 4
+    mark = jnp.full((16, TB), found[3], F32)
+    for k in (2, 1, 0):
+        mark = jnp.where(group == k, found[k], mark)
+    marks[at[0], at[1], at[2]] = mark.astype(BF)
+    own = load(pay, mine.at[at[0], at[1], at[2]], local_sems.at[0])
     me.greet()
-    for copy in own:
-        copy.wait()
+    own.wait()
     wire = Wire(send_sems, recv_sems)
     active = []
     known = set()
@@ -476,7 +484,7 @@
     swaps = [to_sibling(tok, tok_s, wide_sems.at[0]), to_sibling(grad, grad_s, wide_sems.at[1])]
     for swap in swaps:
         swap.start()
-    sums = reduce_parts(me, scale, q, total, scratch[31:])
+    sums = reduce_parts(me, scale, q, total, scratch[33:])
     pieces = [(tok, tok_s, tok2, n) for n in range(D // PIECE)] + [(grad, grad_s, grad2, n) for n in range(FF // PIECE)]
 
     def fetch(k):
@@ -620,22 +628,29 @@
     for swap in swaps:
         swap.wait_send()
     sums[4]()
-
-
-def whole_step(pay, mark, tok, grad, scale):
+    for k in (0, 1):
+        half = slice(k * TB, (k + 1) * TB)
+        left_grad[:, half] = total[k, :LEFT]
+        right_grad[half, :] = total[k, LEFT : LEFT + 2 * TB].T[:, :RIGHT]
+        tile_grad[k] = total[k, LEFT + RIGHT :]
+
+
+def whole_step(rows, cols, left, right, tiles, tok, grad, scale):
     here = tok.shape[0]
     return pl.pallas_call(
         lambda *refs: kernel(scale, *refs),
         out_shape=(
-            jax.ShapeDtypeStruct((2, QROWS, TB), F32),
             jax.ShapeDtypeStruct((here, FF), BF),
             jax.ShapeDtypeStruct((here, D), BF),
+            jax.ShapeDtypeStruct((LEFT, R), F32),
+            jax.ShapeDtypeStruct((R, RIGHT), F32),
+            jax.ShapeDtypeStruct((2, TB, TB), F32),
             jax.ShapeDtypeStruct((2, SIDE, SIDE, SIDE, QROWS, TB), BF),
             jax.ShapeDtypeStruct(tok.shape, BF),
             jax.ShapeDtypeStruct(grad.shape, BF),
         ),
-        in_specs=[ANY] * 4,
-        out_specs=(VMEM,) + (ANY,) * 5,
+        in_specs=[pl.BlockSpec(memory_space=pltpu.SMEM)] * 2 + [VMEM] * 3 + [ANY] * 2,
+        out_specs=(ANY,) * 2 + (VMEM,) * 3 + (ANY,) * 3,
         scratch_shapes=[
             pltpu.VMEM((SIDE, SIDE, SIDE, QROWS, TB), BF),
             pltpu.VMEM((2, SIDE, SIDE, SIDE, LEFT, TB), BF),
@@ -668,6 +683,8 @@
             pltpu.SemaphoreType.DMA((2,)),
             pltpu.SemaphoreType.DMA((2,)),
             pltpu.SemaphoreType.DMA((2, 2)),
+            pltpu.VMEM((QROWS, TB), BF),
+            pltpu.VMEM((2, QROWS, TB), F32),
             pltpu.SemaphoreType.DMA((100,)),
             pltpu.SemaphoreType.DMA((100,)),
         ]
@@ -676,25 +693,14 @@
             collective_id=0, has_side_effects=True, vmem_limit_bytes=63 * 1024 * 1024
         ),
         name="whole_step",
-    )(pay, mark, tok, grad)
+    )(rows, cols, left, right, tiles, tok, grad)
 
 
 def local(tokens, left_factor, right_factor, tile_values, tile_rows, tile_cols, grad_out):
     grad_scale = 1.0 / math.sqrt(tokens.shape[0] * lax.axis_size("fsdp") * lax.axis_size("rep"))
-    mark = jnp.repeat(jnp.concatenate([tile_rows, tile_cols]).astype(BF), 4)
-    mark = jnp.broadcast_to(mark[:, None], (16, TB))
-    pay = jnp.concatenate(
-        [
-            left_factor.reshape(LEFT, 2, TB).transpose(1, 0, 2),
-            right_factor.T.reshape(RIGHT, 2, TB).transpose(1, 0, 2),
-            tile_values,
-        ],
-        1,
+    return tuple(
+        whole_step(tile_rows, tile_cols, left_factor, right_factor, tile_values, tokens, grad_out, grad_scale)[:5]
     )
-    total, out_rows, input_grad, *_ = whole_step(pay, mark, tokens, grad_out, grad_scale)
-    left_grad = total[:, :LEFT].transpose(1, 0, 2).reshape(LEFT, R)
-    right_grad = total[:, LEFT : LEFT + RIGHT].transpose(0, 2, 1).reshape(R, RIGHT)
-    return (out_rows, input_grad, left_grad, right_grad, total[:, LEFT + RIGHT :])
 
 
 def solution(mesh):

time: 142 us -> 136 us (0.958)
  other arithmetic: 2.97 us -> 0 us
  local copies, waits for them, and re-layouts: 11.6 us -> 9.99 us
    unnamed x6 -> x12, local copies, waits for them, and re-layouts: 5.27 us -> 9.99 us
    reshape x2 -> x0, local copies, waits for them, and re-layouts: 3.12 us -> none  [the longest x1 1.64 us: local(): total[:, LEFT:LEFT + RIGHT].transpose(0, 2, 1).reshape(R, RIGHT)]
    concatenate x2 -> x0, other arithmetic: 1.62 us -> none  [the longest x1 1.54 us: local(): jnp.concatenate([left_factor.reshape(LEFT, 2, TB).transpose(1, 0, 2), rig...]
    slice x1 -> x0, local copies, waits for them, and re-layouts: 1.57 us -> none  [local(): total[:, LEFT + RIGHT:]]
where the time goes in v4:
time: 136 us
  Pallas kernels  125 us (92%)
  local copies, waits for them, and re-layouts  9.99 us (7%)
    pallas_call x1, Pallas kernels, whole_step(): pl.pallas_call(lambda *refs: kernel(scale, *refs), out_shape=(jax.ShapeDt...  125 us
    unnamed x12, local copies, waits for them, and re-layouts  9.99 us

profile of v4, /device:TPU:1, one launch (start us, length us, event | category | flops | bytes accessed | tf_op | source)
XLA Modules:
  0.0 135.7 jit_solution(9398510823377452633)
XLA Ops:
  0.6 1.7 %copy.12.refs_3_ = bf16[256,224]{1,0:T(8,128)(2,1)} copy(bf16[256,224]{0,1:T(8,128)(2,1)} %param.9) | data formatting | bytes 229376 | tf_op args[2]
  2.3 125.1 %whole_step.1 = (bf16[128,14336]{1,0:T(8,128)(2,1)}, bf16[128,4096]{1,0:T(8,128)(2,1)}, f32[64,256]{1,0:T(8,128)}, f32[256,224]{1,0:T(8,128)}, f32[2,128,128]{2,...) custom-call(s32[2]{0:T(128)} %refs_0_.1, s32[2]{0:T(128)} %refs_1_.1, ...), custom_call_target="tpu_custom_call" | custom-call | tf_op jit(solution)/shard_map/whole_step/pallas_call | solution.py:640
  127.4 1.8 %copy.13 = f32[256,224]{0,1:T(8,128)} copy(f32[256,224]{1,0:T(8,128)} %get-tuple-element.18) | data formatting | bytes 458752
  129.2 0.0 copy-start
  129.2 0.0 copy-start.2
  129.2 0.0 copy-start.1
  129.2 4.3 %copy.18 = bf16[128,14336]{1,0:T(8,128)(2,1)} copy(bf16[128,14336]{1,0:T(8,128)(2,1)} %get-tuple-element.25) | data formatting | bytes 7340032
  133.5 0.0 copy-done
  133.5 1.0 copy.19
  134.4 0.0 copy-done.2
  134.4 0.6 copy.20
  135.1 0.0 copy-done.1
  135.1 0.7 copy.21
Async XLA Ops:
  129.2 4.3 %copy-start = (bf16[128,4096]{1,0:T(8,128)(2,1)S(1)}, bf16[128,4096]{1,0:T(8,128)(2,1)}, u32[]{:S(2)}) copy-start(bf16[128,4096]{1,0:T(8,128)(2,1)} %get-tuple-element.26) | copy-start | bytes 3145732
  129.2 5.3 %copy-start.2 = (f32[64,256]{1,0:T(8,128)S(1)}, f32[64,256]{1,0:T(8,128)}, u32[]{:S(2)}) copy-start(f32[64,256]{1,0:T(8,128)} %get-tuple-element.27) | copy-start | bytes 196612
  129.2 5.9 %copy-start.1 = (f32[2,128,128]{2,1,0:T(8,128)S(1)}, f32[2,128,128]{2,1,0:T(8,128)}, u32[]{:S(2)}) copy-start(f32[2,128,128]{2,1,0:T(8,128)} %get-tuple-element.29) | copy-start | bytes 393220

commit v5 on v4

--- a/solution.py
+++ b/solution.py
@@ -320,7 +320,7 @@
 CHUNKS = 8
 PER = 64 // CHUNKS
 WIDE = PER * RIGHT
-SLICES = 4
+SLICES = 2
 EMPTY = 128
 PIECE = 2048
 
@@ -586,7 +586,6 @@
         return contract_cols(grad2[within(order[1, 0, t], FF // TB), :here], tile(1, t))
 
     def work():
-        yield
         left_in[1].wait()
         latent_o[...] = dot(wide(tok2, 0, D // TB, here), left[1].reshape(D, TB)).astype(BF)
         tiles_in.wait()
@@ -606,7 +605,8 @@
                 n = j * (WIDE // TB) + b
                 out_v[:, n * TB : (n + 1) * TB] = (dense[:, b * TB : (b + 1) * TB] + run[within(order[0, 3, n], EMPTY + 1)]).astype(BF)
             pltpu.make_async_copy(out_v.at[:, span], out.at[:, span], out_sem).start()
-            yield
+            if j % 2:
+                yield
         for n in range(SLICES):
             running_sums(1, behind, n * 16 // SLICES)
             yield

time: 136 us -> 134 us (0.985)
  Pallas kernels: 125 us -> 123 us
    pallas_call x1, Pallas kernels: 125 us -> 123 us  [whole_step(): pl.pallas_call(lambda *refs: kernel(scale, *refs), out_shape=(jax.ShapeDt...]
where the time goes in v5:
time: 134 us
  Pallas kernels  123 us (92%)
  local copies, waits for them, and re-layouts  9.99 us (7%)
    pallas_call x1, Pallas kernels, whole_step(): pl.pallas_call(lambda *refs: kernel(scale, *refs), out_shape=(jax.ShapeDt...  123 us
    unnamed x12, local copies, waits for them, and re-layouts  9.99 us

profile of v5, /device:TPU:1, one launch (start us, length us, event | category | flops | bytes accessed | tf_op | source)
XLA Modules:
  0.0 134.1 jit_solution(7867120552159142061)
XLA Ops:
  0.6 1.7 %copy.12.refs_3_ = bf16[256,224]{1,0:T(8,128)(2,1)} copy(bf16[256,224]{0,1:T(8,128)(2,1)} %param.9) | data formatting | bytes 229376 | tf_op args[2]
  2.3 123.4 %whole_step.1 = (bf16[128,14336]{1,0:T(8,128)(2,1)}, bf16[128,4096]{1,0:T(8,128)(2,1)}, f32[64,256]{1,0:T(8,128)}, f32[256,224]{1,0:T(8,128)}, f32[2,128,128]{2,...) custom-call(s32[2]{0:T(128)} %refs_0_.1, s32[2]{0:T(128)} %refs_1_.1, ...), custom_call_target="tpu_custom_call" | custom-call | tf_op jit(solution)/shard_map/whole_step/pallas_call | solution.py:640
  125.7 1.8 %copy.13 = f32[256,224]{0,1:T(8,128)} copy(f32[256,224]{1,0:T(8,128)} %get-tuple-element.18) | data formatting | bytes 458752
  127.5 0.0 copy-start
  127.5 0.0 copy-start.2
  127.5 0.0 copy-start.1
  127.5 4.3 %copy.18 = bf16[128,14336]{1,0:T(8,128)(2,1)} copy(bf16[128,14336]{1,0:T(8,128)(2,1)} %get-tuple-element.25) | data formatting | bytes 7340032
  131.8 0.0 copy-done
  131.8 1.0 copy.19
  132.8 0.0 copy-done.2
  132.8 0.6 copy.20
  133.4 0.0 copy-done.1
  133.4 0.7 copy.21
Async XLA Ops:
  127.5 4.3 %copy-start = (bf16[128,4096]{1,0:T(8,128)(2,1)S(1)}, bf16[128,4096]{1,0:T(8,128)(2,1)}, u32[]{:S(2)}) copy-start(bf16[128,4096]{1,0:T(8,128)(2,1)} %get-tuple-element.26) | copy-start | bytes 3145732
  127.5 5.3 %copy-start.2 = (f32[64,256]{1,0:T(8,128)S(1)}, f32[64,256]{1,0:T(8,128)}, u32[]{:S(2)}) copy-start(f32[64,256]{1,0:T(8,128)} %get-tuple-element.27) | copy-start | bytes 196612
  127.5 5.9 %copy-start.1 = (f32[2,128,128]{2,1,0:T(8,128)S(1)}, f32[2,128,128]{2,1,0:T(8,128)}, u32[]{:S(2)}) copy-start(f32[2,128,128]{2,1,0:T(8,128)} %get-tuple-element.29) | copy-start | bytes 393220

commit v6 on v5

--- a/solution.py
+++ b/solution.py
@@ -98,7 +98,7 @@
     return ref.at[sel[0], sel[1], sel[2], pl.ds(r0, n), :]
 
 
-GATHER = (((X, Y, H), 0, 128), ((Y, H, X), 128, 144), ((H, X, Y), 272, 144))
+GATHER = (((X, Y, H), 0, 128), ((Y, H, X), 128, 160), ((H, X, Y), 288, 128))
 
 
 def spread(me, axis, send, got, ready):

time: 134 us -> 132 us (0.985)
  Pallas kernels: 123 us -> 121 us
    pallas_call x1, Pallas kernels: 123 us -> 121 us  [whole_step(): pl.pallas_call(lambda *refs: kernel(scale, *refs), out_shape=(jax.ShapeDt...]
where the time goes in v6:
time: 132 us; the launch traced here: 131 us
  Pallas kernels  121 us (92%)
  local copies, waits for them, and re-layouts  9.99 us (8%)
    pallas_call x1, Pallas kernels, whole_step(): pl.pallas_call(lambda *refs: kernel(scale, *refs), out_shape=(jax.ShapeDt...  121 us
    unnamed x12, local copies, waits for them, and re-layouts  9.99 us

profile of v6, /device:TPU:1, one launch (start us, length us, event | category | flops | bytes accessed | tf_op | source)
XLA Modules:
  0.0 131.5 jit_solution(7365252467973803979)
XLA Ops:
  0.6 1.7 %copy.12.refs_3_ = bf16[256,224]{1,0:T(8,128)(2,1)} copy(bf16[256,224]{0,1:T(8,128)(2,1)} %param.9) | data formatting | bytes 229376 | tf_op args[2]
  2.3 120.8 %whole_step.1 = (bf16[128,14336]{1,0:T(8,128)(2,1)}, bf16[128,4096]{1,0:T(8,128)(2,1)}, f32[64,256]{1,0:T(8,128)}, f32[256,224]{1,0:T(8,128)}, f32[2,128,128]{2,...) custom-call(s32[2]{0:T(128)} %refs_0_.1, s32[2]{0:T(128)} %refs_1_.1, ...), custom_call_target="tpu_custom_call" | custom-call | tf_op jit(solution)/shard_map/whole_step/pallas_call | solution.py:640
  123.1 1.8 %copy.13 = f32[256,224]{0,1:T(8,128)} copy(f32[256,224]{1,0:T(8,128)} %get-tuple-element.18) | data formatting | bytes 458752
  124.9 0.0 copy-start
  124.9 0.0 copy-start.2
  124.9 0.0 copy-start.1
  124.9 4.3 %copy.18 = bf16[128,14336]{1,0:T(8,128)(2,1)} copy(bf16[128,14336]{1,0:T(8,128)(2,1)} %get-tuple-element.25) | data formatting | bytes 7340032
  129.2 0.0 copy-done
  129.2 1.0 copy.19
  130.2 0.0 copy-done.2
  130.2 0.6 copy.20
  130.8 0.0 copy-done.1
  130.8 0.7 copy.21
Async XLA Ops:
  124.9 4.3 %copy-start = (bf16[128,4096]{1,0:T(8,128)(2,1)S(1)}, bf16[128,4096]{1,0:T(8,128)(2,1)}, u32[]{:S(2)}) copy-start(bf16[128,4096]{1,0:T(8,128)(2,1)} %get-tuple-element.26) | copy-start | bytes 3145732
  124.9 5.3 %copy-start.2 = (f32[64,256]{1,0:T(8,128)S(1)}, f32[64,256]{1,0:T(8,128)}, u32[]{:S(2)}) copy-start(f32[64,256]{1,0:T(8,128)} %get-tuple-element.27) | copy-start | bytes 196612
  124.9 5.9 %copy-start.1 = (f32[2,128,128]{2,1,0:T(8,128)S(1)}, f32[2,128,128]{2,1,0:T(8,128)}, u32[]{:S(2)}) copy-start(f32[2,128,128]{2,1,0:T(8,128)} %get-tuple-element.29) | copy-start | bytes 393220
